TPU v7x, 32 devices: a whole 2x2x4 slice. The times are simulated.
32 devices in a mesh: scen: 8 (over z, y), link: 4 (over x, core).
Axes of the slice: x: 2, y: 2, z: 4, core: 2. Of those that a mesh axis runs over, the one named last changes fastest.
Arguments:
- factor_inv: bfloat16 [16, 1024, 1024], P('scen'), may hold values from -0.1875 to 0.1875
- coupling: bfloat16 [16, 1024, 1024], P('scen', None, 'link'), may hold values from -0.375 to 0.375
- first_diag: float32 [128, 128], P('scen'), may hold values from 1 to 10
- pattern: int32 [16, 8], P('scen'), may hold values from 0 to 127, as said below
Outputs:
- panel: float32 [16384, 128], P('scen')
- trailing: float32 [16384, 16384], P('scen', 'link')
Inputs may be any that keep to these rules, and one draw needn't show every extreme that they name: `pattern`: slot t of a scenario names a block of column range t // 2, that is, a block p with p // 32 = t // 2. The 2 scenarios of rows s * 2 to (s + 1) * 2 - 1 name every block at most once among them, and at most 2 blocks of any one group of blocks with the same p // 16. The first scenario of every such set names block 0 in slot 0.
All inputs are finite; a program needn't handle non-finite values.
Results may differ from a plain program's by a relative error of at most 0.0005.
Values may be sent and summed in bfloat16 or wider, within the bound.
A program may use at most 128 MiB of HBM per device.

v0:
```python
import jax
import jax.numpy as jnp
from jax import lax
from jax.sharding import PartitionSpec as P


def broadcast(value, axis, source):
    kept = jnp.where(lax.axis_index(axis) == source, value, 0).astype(value.dtype)
    return lax.psum(kept, axis)


def per_device(factor_inv, coupling, first_diag, pattern):
    tile_size = first_diag.shape[1]
    rows_own = first_diag.shape[0]
    scen_count = lax.axis_size("scen")
    link_count = lax.axis_size("link")
    scen_pos = lax.axis_index("scen")
    link_pos = lax.axis_index("link")
    block_count = rows_own * scen_count
    per_link = block_count // link_count
    col_width = coupling.shape[2]
    slot_count = col_width // tile_size
    own_slabs = jnp.einsum(
        "snm,smc->snc", factor_inv, coupling, preferred_element_type=jnp.float32
    ).astype(jnp.bfloat16)
    contrib = jnp.einsum(
        "snr,snc->src",
        lax.all_gather(own_slabs, "link", axis=2, tiled=True),
        own_slabs,
        preferred_element_type=jnp.float32,
    )
    scen_here = contrib.shape[0]
    spread = pattern.shape[1]
    blocks = pattern.reshape(-1)
    tile_rows = contrib.reshape(scen_here * spread, tile_size, col_width)
    own_cols = (
        lax.dynamic_slice_in_dim(pattern, link_pos * slot_count, slot_count, 1)
        - link_pos * per_link
    )
    col_rows = jnp.broadcast_to(own_cols[:, None, :], (scen_here, spread, slot_count)).reshape(
        scen_here * spread, slot_count
    )
    col_range = jnp.arange(per_link, dtype=jnp.int32)
    picks = scen_here * slot_count
    owners_here = per_link // rows_own
    limit = max(1, (picks + owners_here - 1) // owners_here)
    owners = blocks // rows_own
    listed = jnp.arange(blocks.shape[0], dtype=jnp.int32)
    earlier = (owners[:, None] == owners[None, :]) & (listed[None, :] < listed[:, None])
    rank = jnp.sum(earlier.astype(jnp.int32), axis=1)
    target = owners * limit + rank
    outgoing = (
        jnp.zeros((scen_count * limit, tile_size, col_width), jnp.float32).at[target].set(tile_rows)
    )
    row_labels = jnp.full((scen_count * limit,), -1, jnp.int32).at[target].set(blocks % rows_own)
    col_labels = jnp.full((scen_count * limit, slot_count), -1, jnp.int32).at[target].set(col_rows)
    arrived, arrived_rows, arrived_cols = (
        lax.all_to_all(outgoing, "scen", split_axis=0, concat_axis=0, tiled=True),
        lax.all_to_all(row_labels, "scen", split_axis=0, concat_axis=0, tiled=True),
        lax.all_to_all(col_labels, "scen", split_axis=0, concat_axis=0, tiled=True),
    )
    row_pick = (arrived_rows[:, None] == jnp.arange(rows_own, dtype=jnp.int32)[None, :]).astype(
        jnp.float32
    )
    col_pick = (arrived_cols[:, :, None] == col_range[None, None, :]).astype(jnp.float32)
    weight = row_pick[:, :, None, None] * col_pick[:, None, :, :]
    arrived = arrived.reshape(scen_count * limit, tile_size, slot_count, tile_size)
    summed = jnp.einsum("nrkq,nxky->rxqy", weight, arrived, precision=lax.Precision.HIGHEST)
    global_rows = scen_pos * rows_own + jnp.arange(rows_own, dtype=jnp.int32)
    global_cols = link_pos * per_link + col_range
    on_diagonal = (global_rows[:, None] == global_cols[None, :]).astype(jnp.float32)
    unit_matrix = jnp.eye(tile_size, dtype=jnp.float32)
    diag_part = (
        on_diagonal[:, None, :, None]
        * (first_diag[:, :, None] * unit_matrix[None, :, :])[:, :, None, :]
    )
    schur = (summed + diag_part).reshape(rows_own * tile_size, per_link * tile_size)
    corner = broadcast(schur[:tile_size, :tile_size], "scen", 0)
    lead_factor = jnp.linalg.cholesky(corner)
    solved = jax.scipy.linalg.solve_triangular(lead_factor, schur[:, :tile_size].T, lower=True).T
    top_block = jnp.where(scen_pos == 0, lead_factor, solved[:tile_size])
    panel_mine = broadcast(jnp.concatenate([top_block, solved[tile_size:]], axis=0), "link", 0)
    gathered = lax.all_gather(panel_mine, "scen", axis=0, tiled=True)
    partner = lax.dynamic_slice_in_dim(
        gathered, link_pos * per_link * tile_size, per_link * tile_size, 0
    )
    trailing = schur - jnp.dot(
        panel_mine, partner.T, precision=lax.Precision.HIGHEST, preferred_element_type=jnp.float32
    )
    return (panel_mine, trailing)


def solution(mesh):
    in_specs = (P("scen", None, None), P("scen", None, "link"), P("scen", None), P("scen", None))
    out_specs = (P("scen", None), P("scen", "link"))
    return jax.shard_map(
        per_device, mesh=mesh, in_specs=in_specs, out_specs=out_specs, check_vma=False
    )
```

profile of v0, /device:TPU:0, one launch (start us, length us, event | category | flops | bytes accessed | tf_op | source)
XLA Modules:
  0.0 517.7 jit_solution(12495140166308132009)
XLA Ops:
  7.2 1.2 copy-done
  8.4 4.4 convolution_convert_fusion
  14.5 7.3 %all-to-all-start.1 = ((s32[8,2,1]{1,2,0:T(1,128)}), s32[8,2,1]{1,2,0:T(1,128)S(1)}, u32[]{:S(2)}, u32[]{:S(2)}) async-start(s32[8,2,1]{1,2,0:T(1,128)} %bitcast.5), calls=%async_computation.1 | async-start | bytes 8192 | tf_op jit(solution)/shard_map/all_to_all | solution.py:59
  23.2 27.5 %all-gather.3.cloned.1.call-done = bf16[2,1024,1024]{2,1,0:T(8,128)(2,1)} async-done(((bf16[2,1024,256]{2,1,0:T(8,128)(2,1)}), bf16[2,1024,1024]{2,1,0:T(8,128)(2,1)}) %all-gather.3.cloned.1.call-update) | async-done | bytes 4194320 | tf_op jit(solution)/shard_map/all_gather | solution.py:28
  50.7 4.2 fusion.21
  54.9 5.5 %all-to-all-start.2 = ((s32[8,2,2]{1,2,0:T(2,128)}), s32[8,2,2]{1,2,0:T(2,128)S(1)}, u32[]{:S(2)}, u32[]{:S(2)}) async-start(s32[8,2,2]{1,2,0:T(2,128)} %copy.47), calls=%async_computation.2 | async-start | bytes 16384 | tf_op jit(solution)/shard_map/all_to_all | solution.py:60
  60.5 1.5 broadcast_in_dim.13
  62.0 3.7 scatter_fusion
  65.7 1.3 all-to-all-done.2
  67.0 4.7 all-to-all-start
  73.9 45.9 %all-to-all-done = f32[16,128,256]{2,1,0:T(8,128)S(1)} async-done(((f32[16,128,256]{2,1,0:T(8,128)}), f32[16,128,256]{2,1,0:T(8,128)S(1)}, u32[]{:S(2)}, u32[]{:S(2)}) %all-to-all-start) | async-done | bytes 2097184 | tf_op jit(solution)/shard_map/all_to_all | solution.py:58
  119.8 1.8 copy.42
  121.6 2.4 copy.54
  124.0 32.0 %bitcast_add_fusion = f32[16,128,32,128]{3,2,0,1:T(8,128)} fusion(f32[16,128,128]{2,0,1:T(8,128)S(1)} %broadcast_multiply_fusion, f32[16,32]{1,0:T(8,128)S(1)} %compare_convert_fusion, f32[16,128,2,128,1]{3,0,2,4,1:T(8,128)S(1)} %copy.54, f32[16,2,32]{2,0,1:T(8,128)S(1)} %fusion.10, f32[16,16]{0,1:T(8,128)S(1)} %fusion.14), kind=kOutput, calls=%fused_computation.4 | convolution fusion | flops 3238019072 | bytes 36707328 | tf_op jit(solution)/shard_map/nrkq,nxky->rxqy/dot_general | solution.py:68
  156.0 13.1 %copy.51 = f32[16,128,32,128]{3,2,1,0:T(8,128)S(1)} copy(f32[16,128,32,128]{3,2,0,1:T(8,128)} %bitcast_add_fusion) | data formatting | bytes 67108864 | tf_op jit(solution)/shard_map/add | solution.py:77
  169.1 37.9 %copy.66 = f32[256,8,32,128]{3,1,2,0:T(8,128)} copy(f32[256,8,32,128]{3,2,1,0:T(8,128)S(1)} %bitcast.51) | data formatting | bytes 67108864
  207.0 1.5 slice_select_fusion.1
  208.6 66.7 %all-reduce.3.cloned.1.call-done = f32[128,128]{1,0:T(8,128)} async-done(((f32[128,128]{1,0:T(8,128)}), f32[128,128]{1,0:T(8,128)}) %all-reduce.3.cloned.1.call-update) | async-done | bytes 65552 | tf_op jit(solution)/shard_map/psum | solution.py:9
  277.0 11.7 %cholesky.19 = f32[128,128]{1,0:T(8,128)S(1)} custom-call(f32[128,128]{1,0:T(8,128)S(1)} %fusion.8), custom_call_target="Cholesky" | custom-call | tf_op jit(solution)/shard_map/jit(cholesky)/cholesky | solution.py:79
  290.1 9.8 %custom-call.7 = f32[1,128,128]{1,2,0:T(8,128)S(1)} custom-call(f32[1,128,128]{2,1,0:T(8,128)S(1)} %select_bitcast_fusion), custom_call_target="InvertDiagBlocksLowerTriangular" | custom-call | tf_op jit(solution)/shard_map/jit(_solve_triangular)/triangular_solve | solution.py:80
  299.9 2.2 fusion.1
  304.0 36.1 %all-reduce.5.cloned.1.call-done = f32[2048,128]{1,0:T(8,128)} async-done(((f32[2048,128]{1,0:T(8,128)}), f32[2048,128]{1,0:T(8,128)}) %all-reduce.5.cloned.1.call-update) | async-done | bytes 1048592 | tf_op jit(solution)/shard_map/psum | solution.py:9
  340.1 127.5 %all-gather.5.cloned.1.call-done = f32[16384,128]{1,0:T(8,128)} async-done(((f32[2048,128]{1,0:T(8,128)}), f32[16384,128]{1,0:T(8,128)}) %all-gather.5.cloned.1.call-update) | async-done | bytes 8388624 | tf_op jit(solution)/shard_map/all_gather | solution.py:83
  467.6 42.6 %convolution_subtract_fusion = f32[2048,4096]{1,0:T(8,128)} fusion(f32[2048,128]{1,0:T(8,128)} %all-reduce.5.cloned.1.call-done, f32[16384,128]{1,0:T(8,128)} %all-gather.5.cloned.1.call-done, s32[]{:T(128)S(6)} %select_n.83, f32[256,8,32,128]{3,2,1,0:T(8,128)} %bitcast.52), kind=kOutput, calls=%fused_computation.5 | convolution fusion | flops 12893290496 | bytes 70254592 | tf_op jit(solution)/shard_map/dot_general | solution.py:87
  (52 shorter events, 11.3 us)
Async XLA Ops:
  7.2 1.2 copy-start
  7.2 5.6 %copy-start.5 = (s32[2,8]{1,0:T(2,128)S(1)}, s32[2,8]{1,0:T(2,128)}, u32[]{:S(2)}) copy-start(s32[2,8]{1,0:T(2,128)} %param.7) | copy-start | bytes 196
  7.2 43.5 %all-gather.3.cloned.1.call-start = ((), (), s32[]{:S(2)}) async-start(), calls=%async_computation.3 | async-start | bytes 5242880 | tf_op jit(solution)/shard_map/all_gather | solution.py:28
  14.5 40.4 %all-to-all-start.1 = ((s32[8,2,1]{1,2,0:T(1,128)}), s32[8,2,1]{1,2,0:T(1,128)S(1)}, u32[]{:S(2)}, u32[]{:S(2)}) async-start(s32[8,2,1]{1,2,0:T(1,128)} %bitcast.5), calls=%async_computation.1 | async-start | bytes 8192 | tf_op jit(solution)/shard_map/all_to_all | solution.py:59
  54.9 12.0 %all-to-all-start.2 = ((s32[8,2,2]{1,2,0:T(2,128)}), s32[8,2,2]{1,2,0:T(2,128)S(1)}, u32[]{:S(2)}, u32[]{:S(2)}) async-start(s32[8,2,2]{1,2,0:T(2,128)} %copy.47), calls=%async_computation.2 | async-start | bytes 16384 | tf_op jit(solution)/shard_map/all_to_all | solution.py:60
  62.0 9.9 %copy-start.4 = (f32[16,128]{1,0:T(8,128)S(1)}, f32[16,128]{1,0:T(8,128)}, u32[]{:S(2)}) copy-start(f32[16,128]{1,0:T(8,128)} %param.6) | copy-start | bytes 24580
  67.0 52.8 %all-to-all-start = ((f32[16,128,256]{2,1,0:T(8,128)}), f32[16,128,256]{2,1,0:T(8,128)S(1)}, u32[]{:S(2)}, u32[]{:S(2)}) async-start(f32[16,128,256]{2,1,0:T(8,128)} %scatter_fusion), calls=%async_computation | async-start | bytes 4194304 | tf_op jit(solution)/shard_map/all_to_all | solution.py:58
  71.7 203.6 %all-reduce.3.cloned.1.call-start = ((), (), s32[]{:S(2)}) async-start(), calls=%async_computation.4 | async-start | bytes 131072 | tf_op jit(solution)/shard_map/psum | solution.py:9
  169.1 37.9 %copy-start.2 = (f32[16,128,32,128]{3,2,1,0:T(8,128)}, f32[16,128,32,128]{3,2,1,0:T(8,128)S(1)}, u32[]{:S(2)}) copy-start(f32[16,128,32,128]{3,2,1,0:T(8,128)S(1)} %copy.51) | copy-start | bytes 100663296
  208.5 131.6 %all-reduce.5.cloned.1.call-start = ((), (), s32[]{:S(2)}) async-start(), calls=%async_computation.5 | async-start | bytes 2097152 | tf_op jit(solution)/shard_map/psum | solution.py:9
  303.9 163.7 %all-gather.5.cloned.1.call-start = ((), (), s32[]{:S(2)}) async-start(), calls=%async_computation.6 | async-start | bytes 9437184 | tf_op jit(solution)/shard_map/all_gather | solution.py:83
  340.1 170.1 %copy-start.3 = (f32[2048,128]{1,0:T(8,128)S(1)}, f32[2048,128]{1,0:T(8,128)}, u32[]{:S(2)}) copy-start(f32[2048,128]{1,0:T(8,128)} %all-reduce.5.cloned.1.call-done) | copy-start | bytes 3145732
  467.6 43.5 %copy-start.1 = (bf16[2,1024,256]{2,1,0:T(8,128)(2,1)S(1)}, bf16[2,1024,256]{2,1,0:T(8,128)(2,1)}, u32[]{:S(2)}) copy-start(bf16[2,1024,256]{2,1,0:T(8,128)(2,1)} %param.5) | copy-start | bytes 3145732
Sparse Core Ops, SparseCore 0:
  12.9 37.7 all-gather.2
  208.6 66.5 all-reduce.2
  304.0 35.9 all-reduce.4
  342.3 125.3 all-gather.4
where the time goes:
time: 518 us
  waiting for transfers between devices  305 us (59%)
  matrix products  85.4 us (16%)
  local copies, waits for them, and re-layouts  67.1 us (13%)
  other arithmetic  28.3 us (5%)
  starting transfers between devices  17.9 us (3%)
  between operations  14 us (3%)
    all_gather x1, waiting for transfers between devices, per_device(): gathered = lax.all_gather(panel_mine, 'scen', axis=0, tiled=True)  128 us
    psum x2, waiting for transfers between devices, broadcast(): return lax.psum(kept, axis)  103 us
    all_to_all x1, waiting for transfers between devices, per_device(): lax.all_to_all(outgoing, 'scen', split_axis=0, concat_axis=0, tiled=True)  45.9 us
    dot_general x1, matrix products, per_device(): jnp.dot(panel_mine, partner.T, precision=lax.Precision.HIGHEST, preferred...  42.6 us
    unnamed x15, local copies, waits for them, and re-layouts  40.2 us
    dot_general x1, matrix products, per_device(): jnp.einsum('nrkq,nxky->rxqy', weight, arrived, precision=lax.Precision.HI...  32 us
    all_gather x1, waiting for transfers between devices, per_device(): lax.all_gather(own_slabs, 'link', axis=2, tiled=True)  27.5 us
    add x1, local copies, waits for them, and re-layouts, per_device(): summed + diag_part  13.1 us
  transfers between devices with their start and end apart: 7, of which 6 were waited for; matrix products, arithmetic and copies ran while one was open for 3% of the time, Pallas kernels for 0%

commit v1 on v0

v1 whole, which is shorter than its diff:
```python
import functools

import jax
import jax.numpy as jnp
from jax import lax
from jax.experimental import pallas as pl
from jax.experimental.pallas import tpu as pltpu
from jax.sharding import PartitionSpec as P

F32 = jnp.float32
BF16 = jnp.bfloat16
HIGHEST = lax.Precision.HIGHEST


def factor(work):
    size = work.shape[0]
    inverse = (
        lax.broadcasted_iota(jnp.int32, (size, size), 0)
        == lax.broadcasted_iota(jnp.int32, (size, size), 1)
    ).astype(F32)
    upper_rows, inverse_rows = [], []
    base = 0
    for j in range(size):
        start = j // 8 * 8
        if start > base:
            work, inverse, base = work[start - base :], inverse[start - base :], start
        k = j - base
        column = work[:, j : j + 1]
        pivot = column[k : k + 1]
        row, inverse_row = work[k : k + 1], inverse[k : k + 1]
        scale = 1.0 / jnp.sqrt(pivot)
        upper_rows.append(row * scale)
        inverse_rows.append(inverse_row * scale)
        if j + 1 < size:
            below = lax.broadcasted_iota(jnp.int32, (size - base, 1), 0) > k
            ratio = jnp.where(below, column * (1.0 / pivot), 0.0)
            work = work - ratio * row
            inverse = inverse - ratio * inverse_row
    return jnp.concatenate(upper_rows, axis=0), jnp.concatenate(inverse_rows, axis=0)


def factor_kernel(corner_ref, lower_ref, inverse_ref):
    upper, inverse = factor(corner_ref[...])
    size = upper.shape[0]
    keep = lax.broadcasted_iota(jnp.int32, (size, size), 0) <= lax.broadcasted_iota(
        jnp.int32, (size, size), 1
    )
    lower_ref[...] = jnp.where(keep, upper, 0.0).T
    inverse_ref[...] = inverse


def lead_factor(corner):
    size = corner.shape[0]
    shape = jax.ShapeDtypeStruct((size, size), F32)
    return pl.pallas_call(
        factor_kernel,
        out_shape=(shape, shape),
        name="lead_factor",
        compiler_params=pltpu.CompilerParams(vmem_limit_bytes=32 * 2**20),
    )(corner)


def split(value):
    high = value.astype(BF16)
    return high, (value - high.astype(F32)).astype(BF16)


def finish_kernel(
    place_ref,
    row_label_ref,
    col_label_ref,
    lead_label_ref,
    arrived_ref,
    lead_ref,
    column_ref,
    lower_ref,
    inverse_ref,
    diag_ref,
    panel_ref,
    trailing_ref,
    partner_ref,
    raw_ref,
):
    tile = lower_ref.shape[0]
    width = trailing_ref.shape[1]
    slots = arrived_ref.shape[2] // tile
    row = pl.program_id(0)
    rows_own = pl.num_programs(0)
    global_row = place_ref[0] * rows_own + row
    first_col = place_ref[1] * (width // tile)
    chunk = 512

    @pl.when(row == 0)
    def _():
        raw_ref[...] = jnp.zeros_like(raw_ref)
        for source in range(lead_ref.shape[0]):
            for slot in range(slots):
                at = pl.multiple_of(lead_label_ref[source * slots + slot] * tile, tile)
                raw_ref[:, pl.ds(at, tile)] += lead_ref[source, :, slot * tile : (slot + 1) * tile]

        @pl.loop(0, width // chunk)
        def _(step):
            at = pl.ds(pl.multiple_of(step * chunk, chunk), chunk)
            high, low = split(
                jnp.dot(
                    inverse_ref[...], raw_ref[:, at], precision=HIGHEST, preferred_element_type=F32
                )
            )
            partner_ref[:tile, at] = high
            partner_ref[tile : 2 * tile, at] = high
            partner_ref[2 * tile :, at] = low

        @pl.when(first_col == 0)
        def _():
            high, low = split(lower_ref[...].T)
            partner_ref[:tile, :tile] = high
            partner_ref[tile : 2 * tile, :tile] = high
            partner_ref[2 * tile :, :tile] = low

    solved = lax.dot_general(
        column_ref[...],
        inverse_ref[...],
        (((1,), (1,)), ((), ())),
        precision=HIGHEST,
        preferred_element_type=F32,
    )
    mine = jnp.where(global_row == 0, lower_ref[...], solved)
    panel_ref[...] = mine
    high, low = split(-mine)
    left = jnp.concatenate([high, low, high], axis=1)
    for step in range(width // chunk):
        at = slice(step * chunk, (step + 1) * chunk)
        trailing_ref[:, at] = jnp.dot(left, partner_ref[:, at], preferred_element_type=F32)

    @pl.loop(0, arrived_ref.shape[0])
    def _(listed):
        @pl.when(row_label_ref[listed] == row)
        def _():
            for slot in range(slots):
                at = pl.multiple_of(col_label_ref[listed * slots + slot] * tile, tile)
                trailing_ref[:, pl.ds(at, tile)] += arrived_ref[
                    listed, :, slot * tile : (slot + 1) * tile
                ]

    on_col = global_row - first_col

    @pl.when((on_col >= 0) & (on_col < width // tile))
    def _():
        at = pl.multiple_of(on_col * tile, tile)
        unit = lax.broadcasted_iota(jnp.int32, (tile, tile), 0) == lax.broadcasted_iota(
            jnp.int32, (tile, tile), 1
        )
        trailing_ref[:, pl.ds(at, tile)] += jnp.where(unit, diag_ref[pl.ds(row, 1), :], 0.0)


def finish(place, row_labels, col_labels, lead_labels, arrived, lead, column, lower, inverse, diag, width):
    tile = lower.shape[0]
    rows_own = diag.shape[0]
    whole = pl.BlockSpec(memory_space=pltpu.VMEM)
    return pl.pallas_call(
        finish_kernel,
        grid_spec=pltpu.PrefetchScalarGridSpec(
            num_scalar_prefetch=4,
            grid=(rows_own,),
            in_specs=[
                whole,
                whole,
                pl.BlockSpec((tile, tile), lambda r, *_: (r, 0)),
                whole,
                whole,
                whole,
            ],
            out_specs=[
                pl.BlockSpec((tile, tile), lambda r, *_: (r, 0)),
                pl.BlockSpec((tile, width), lambda r, *_: (r, 0)),
            ],
            scratch_shapes=[pltpu.VMEM((3 * tile, width), BF16), pltpu.VMEM((tile, width), F32)],
        ),
        out_shape=(
            jax.ShapeDtypeStruct((rows_own * tile, tile), F32),
            jax.ShapeDtypeStruct((rows_own * tile, width), F32),
        ),
        name="finish",
        compiler_params=pltpu.CompilerParams(vmem_limit_bytes=48 * 2**20),
    )(place, row_labels, col_labels, lead_labels, arrived, lead, column, lower, inverse, diag)


def per_device(factor_inv, coupling, first_diag, pattern):
    rows_own, tile = first_diag.shape
    scen_count = lax.axis_size("scen")
    link_count = lax.axis_size("link")
    scen_pos = lax.axis_index("scen")
    link_pos = lax.axis_index("link")
    per_link = rows_own * scen_count // link_count
    scen_here, spread = pattern.shape
    width = coupling.shape[2]
    slots = width // tile

    own = jnp.einsum("snm,smc->snc", factor_inv, coupling, preferred_element_type=F32).astype(BF16)
    patterns = lax.all_gather(pattern, "scen", axis=0, tiled=False)

    share = lax.dot_general(
        own[0, :, :tile], own[0, :, :tile], (((0,), (0,)), ((), ())), preferred_element_type=F32
    )
    unit = jnp.eye(tile, dtype=F32)
    share = share + jnp.where(scen_pos == 0, first_diag[0][:, None] * unit, 0.0)
    corner = lax.psum(jnp.where(link_pos == 0, share, 0.0), ("scen", "link"))
    lower, inverse = lead_factor(corner)

    contrib = jnp.einsum(
        "snr,snc->src",
        lax.all_gather(own, "link", axis=2, tiled=True),
        own,
        preferred_element_type=F32,
    ).reshape(scen_here * spread, tile, width)

    picks = scen_here * slots
    owners_here = per_link // rows_own if per_link >= rows_own else 1
    limit = max(1, (picks + owners_here - 1) // owners_here)
    listed = jnp.arange(scen_here * spread, dtype=jnp.int32)
    blocks = patterns.reshape(scen_count, scen_here * spread)
    owners = blocks // rows_own
    earlier = (owners[:, :, None] == owners[:, None, :]) & (listed[None, :] < listed[:, None])
    rank = jnp.sum(earlier.astype(jnp.int32), axis=2)
    target = owners * limit + rank
    places = jnp.arange(scen_count * limit, dtype=jnp.int32)
    hit = target[:, :, None] == places[None, None, :]
    at_place = jnp.sum(jnp.where(hit, listed[None, :, None] + 1, 0), axis=1) - 1
    mine = lax.dynamic_index_in_dim(at_place, scen_pos, 0, keepdims=False)
    outgoing = contrib[jnp.maximum(mine, 0)]
    to_me = lax.dynamic_slice_in_dim(at_place, scen_pos * limit, limit, 1)
    chosen = jnp.maximum(to_me, 0)
    block_here = jnp.take_along_axis(blocks, chosen, axis=1)
    row_labels = jnp.where(to_me >= 0, block_here - scen_pos * rows_own, -1).reshape(-1)
    own_cols = (
        lax.dynamic_slice_in_dim(patterns, link_pos * slots, slots, 2) - link_pos * per_link
    )
    col_labels = jnp.take_along_axis(own_cols, (chosen // spread)[:, :, None], axis=1).reshape(-1)
    lead_labels = own_cols[:, 0, :].reshape(-1)

    arrived = lax.all_to_all(outgoing, "scen", split_axis=0, concat_axis=0, tiled=True)
    lead = lax.all_gather(contrib[0], "scen", axis=0, tiled=False)

    first_col = col_labels.reshape(-1, slots)[:, 0] == 0
    pick = (
        (row_labels[:, None] == jnp.arange(rows_own, dtype=jnp.int32)[None, :])
        & first_col[:, None]
        & (link_pos == 0)
    )
    spot = jnp.sum(pick.astype(jnp.int32), axis=0)
    column = jnp.einsum(
        "nr,nxy->rxy", pick.astype(F32), arrived[:, :, :tile], precision=HIGHEST
    ).reshape(rows_own * tile, tile)
    del spot
    column = lax.psum(column, "link")

    place = jnp.stack([scen_pos, link_pos]).astype(jnp.int32)
    return finish(
        place, row_labels, col_labels, lead_labels, arrived, lead, column, lower, inverse, first_diag,
        per_link * tile,
    )


def solution(mesh):
    in_specs = (P("scen", None, None), P("scen", None, "link"), P("scen", None), P("scen", None))
    out_specs = (P("scen", None), P("scen", "link"))
    return jax.shard_map(
        per_device, mesh=mesh, in_specs=in_specs, out_specs=out_specs, check_vma=False
    )
```

time: 518 us -> 287 us (0.55)
  waiting for transfers between devices: 305 us -> 180 us
  matrix products: 85.4 us -> 11.8 us
  local copies, waits for them, and re-layouts: 67.1 us -> 12 us
  Pallas kernels: 0 us -> 37.5 us
  other arithmetic: 28.3 us -> 1.04 us
  blocking collectives: 0 us -> 22.3 us
  starting transfers between devices: 17.9 us -> 5.68 us
    all_gather x2, waiting for transfers between devices: 155 us -> 15.1 us  [the longest x1 15 us: per_device(): lax.all_gather(own, 'link', axis=2, tiled=True)]
    dot_general x4, matrix products: 83.2 us -> 11.8 us  [the longest x1 4.41 us: per_device(): jnp.einsum('snm,smc->snc', factor_inv, coupling, preferred_element_type=F32)]
    pallas_call x0 -> x2, Pallas kernels: none -> 37.5 us  [the longest x1 26.7 us: finish(): pl.pallas_call(finish_kernel, grid_spec=pltpu.PrefetchScalarGridSpec(num_...]
    unnamed x15 -> x14, local copies, waits for them, and re-layouts: 40.2 us -> 4.47 us
    another operation x5 -> x1, other arithmetic: 22.9 us -> 0.08 us  [per_device(): place = jnp.stack([scen_pos, link_pos]).astype(jnp.int32)]
    all_gather x0 -> x1, blocking collectives: none -> 22.3 us  [per_device(): patterns = lax.all_gather(pattern, 'scen', axis=0, tiled=False)]
    add x1 -> x0, local copies, waits for them, and re-layouts: 13.1 us -> none  [per_device(): summed + diag_part]
    all_to_all x2 -> x0, starting transfers between devices: 12.8 us -> none  [the longest x1 7.29 us: per_device(): lax.all_to_all(row_labels, 'scen', split_axis=0, concat_axis=0, tiled=True)]
  transfers between devices with their start and end apart: 7 -> 5, of which waited for: 6 -> 4; matrix products, arithmetic and copies ran while one was open for 3% -> 3% of each run, Pallas kernels for 0% -> 4%
where the time goes in v1:
time: 287 us; the launch traced here: 286 us
  waiting for transfers between devices  180 us (63%)
  Pallas kernels  37.5 us (13%)
  blocking collectives  22.3 us (8%)
  between operations  15.7 us (5%)
  local copies, waits for them, and re-layouts  12 us (4%)
  matrix products  11.8 us (4%)
  starting transfers between devices  5.68 us (2%)
    psum x1, waiting for transfers between devices, per_device(): corner = lax.psum(jnp.where(link_pos == 0, share, 0.0), ('scen', 'link'))  81.3 us
    all_to_all x1, waiting for transfers between devices, per_device(): lax.all_to_all(outgoing, 'scen', split_axis=0, concat_axis=0, tiled=True)  55.5 us
    psum x1, waiting for transfers between devices, per_device(): column = lax.psum(column, 'link')  28.6 us
    pallas_call x1, Pallas kernels, finish(): pl.pallas_call(finish_kernel, grid_spec=pltpu.PrefetchScalarGridSpec(num_...  26.7 us
    all_gather x1, blocking collectives, per_device(): patterns = lax.all_gather(pattern, 'scen', axis=0, tiled=False)  22.3 us
    all_gather x1, waiting for transfers between devices, per_device(): lax.all_gather(own, 'link', axis=2, tiled=True)  15 us
    pallas_call x1, Pallas kernels, lead_factor(): pl.pallas_call(factor_kernel, out_shape=(shape, shape), name='lead_factor...  10.7 us
  transfers between devices with their start and end apart: 5, of which 4 were waited for; matrix products, arithmetic and copies ran while one was open for 3% of the time, Pallas kernels for 4%

profile of v1, /device:TPU:0, one launch (start us, length us, event | category | flops | bytes accessed | tf_op | source)
XLA Modules:
  0.0 286.4 jit_solution(10619154164677651599)
XLA Ops:
  8.1 1.2 copy-done
  9.2 4.4 %convolution_convert_fusion = bf16[2,1024,256]{2,1,0:T(8,128)(2,1)} fusion(bf16[2,1024,1024]{2,1,0:T(8,128)(2,1)} %param.4, bf16[2,1024,256]{2,1,0:T(8,128)(2,1)S(1)} %copy-done), kind=kOutput, calls=%fused_computation.3 | convolution fusion | flops 1074266112 | bytes 6291456 | tf_op jit(solution)/shard_map/snm,smc->snc/dot_general | solution.py:199
  13.7 22.3 %all-gather.1 = s32[8,2,8]{2,1,0:T(2,128)S(1)} all-gather(s32[1,2,8]{2,1,0:T(2,128)S(1)} %bitcast.32), channel_id=2, replica_groups=mesh['scen'=8,'link'=4] {'scen'}, dimensions={0}, use_global_device_ids=true | all-gather | bytes 576 | tf_op jit(solution)/shard_map/all_gather | solution.py:200
  36.0 0.3 convert_reduce_fusion
  36.5 15.0 %all-gather.5.cloned.1.call-done = bf16[2,1024,1024]{2,1,0:T(8,128)(2,1)} async-done(((bf16[2,1024,256]{2,1,0:T(8,128)(2,1)}), bf16[2,1024,1024]{2,1,0:T(8,128)(2,1)}) %all-gather.5.cloned.1.call-update) | async-done | bytes 4194320 | tf_op jit(solution)/shard_map/all_gather | solution.py:212
  51.5 4.2 %fusion.17 = f32[2,1024,256]{2,1,0:T(8,128)S(1)} fusion(bf16[2,1024,1024]{2,1,0:T(8,128)(2,1)} %all-gather.5.cloned.1.call-done, bf16[2,1024,256]{2,1,0:T(8,128)(2,1)} %convolution_convert_fusion), kind=kOutput, calls=%fused_computation.55 | convolution fusion | flops 1073741824 | bytes 7340032 | tf_op jit(solution)/shard_map/snr,snc->src/dot_general | solution.py:210
  55.8 2.0 gather_fusion
  57.8 5.5 %all-to-all-start = ((f32[16,128,256]{2,1,0:T(8,128)}), f32[16,128,256]{2,1,0:T(8,128)S(1)}, u32[]{:S(2)}, u32[]{:S(2)}) async-start(f32[16,128,256]{2,1,0:T(8,128)} %gather_fusion), calls=%async_computation | async-start | bytes 4194304 | tf_op jit(solution)/shard_map/all_to_all | solution.py:241
  63.4 2.0 fusion
  65.4 1.6 slice.32
  67.8 0.7 gather_fusion.1
  68.8 0.6 gather_fusion.2
  69.4 0.2 fusion.8
  69.6 55.5 %all-to-all-done.arrived_ref = f32[16,128,256]{2,1,0:T(8,128)S(1)} async-done(((f32[16,128,256]{2,1,0:T(8,128)}), f32[16,128,256]{2,1,0:T(8,128)S(1)}, u32[]{:S(2)}, u32[]{:S(2)}) %all-to-all-start) | async-done | bytes 2097184 | tf_op jit(solution)/shard_map/all_to_all | solution.py:241
  125.2 1.2 fusion.1
  126.4 1.3 copy.41
  128.0 0.1 copy.38
  128.3 81.3 %all-reduce.5.cloned.1.call-done.corner_ref = f32[128,128]{1,0:T(8,128)} async-done(((f32[128,128]{1,0:T(8,128)}), f32[128,128]{1,0:T(8,128)}) %all-reduce.5.cloned.1.call-update) | async-done | bytes 65552 | tf_op jit(solution)/shard_map/psum | solution.py:207
  209.6 0.8 copy-done.3
  210.4 10.7 %lead_factor.1 = (f32[128,128]{1,0:T(8,128)S(1)}, f32[128,128]{1,0:T(8,128)S(1)}) custom-call(f32[128,128]{1,0:T(8,128)S(1)} %copy-done.3), custom_call_target="tpu_custom_call" | custom-call | tf_op jit(solution)/shard_map/lead_factor/pallas_call | solution.py:55
  221.2 28.6 %all-reduce.3.cloned.1.call-done.column_ref = f32[2048,128]{1,0:T(8,128)} async-done(((f32[2048,128]{1,0:T(8,128)}), f32[2048,128]{1,0:T(8,128)}) %all-reduce.3.cloned.1.call-update) | async-done | bytes 1048592 | tf_op jit(solution)/shard_map/psum | solution.py:255
  249.8 1.2 copy-done.1
  251.0 1.2 copy-done.2
  252.2 26.7 %finish.1 = (f32[2048,128]{1,0:T(8,128)}, f32[2048,4096]{1,0:T(8,128)}) custom-call(s32[2]{0:T(128)S(1)} %pad_add_fusion.place_ref, s32[16]{0:T(128)S(1)} %reshape.142.row_label_ref, s32[32]{0:T(128)S(1)} %select_n.88.col_label_ref, s32[16]{0:T(128)S(1)} %reshape_squeeze.3.lead_label_ref, f32[16,128,256]{2,1,0:T(8,128)S(1)} %all-to-all-done.arrived_ref, ...), custom_call_target="tpu_custom_call" | custom-call | tf_op jit(solution)/shard_map/finish/pallas_call | solution.py:160
  (50 shorter events, 2.1 us)
Async XLA Ops:
  8.0 1.2 copy-start
  8.0 5.7 %copy-start.6 = (s32[2,8]{1,0:T(2,128)S(1)}, s32[2,8]{1,0:T(2,128)}, u32[]{:S(2)}) copy-start(s32[2,8]{1,0:T(2,128)} %param.7) | copy-start | bytes 196
  8.0 43.5 %all-gather.5.cloned.1.call-start = ((), (), s32[]{:S(2)}) async-start(), calls=%async_computation.1 | async-start | bytes 5242880 | tf_op jit(solution)/shard_map/all_gather | solution.py:212
  55.8 2.0 copy-start.5
  55.8 7.6 %copy-start.4 = (f32[16,128]{1,0:T(8,128)S(1)}, f32[16,128]{1,0:T(8,128)}, u32[]{:S(2)}) copy-start(f32[16,128]{1,0:T(8,128)} %diag_ref.1) | copy-start | bytes 24580
  57.8 67.3 %all-to-all-start = ((f32[16,128,256]{2,1,0:T(8,128)}), f32[16,128,256]{2,1,0:T(8,128)S(1)}, u32[]{:S(2)}, u32[]{:S(2)}) async-start(f32[16,128,256]{2,1,0:T(8,128)} %gather_fusion), calls=%async_computation | async-start | bytes 4194304 | tf_op jit(solution)/shard_map/all_to_all | solution.py:241
  63.3 146.3 %all-reduce.5.cloned.1.call-start = ((), (), s32[]{:S(2)}) async-start(), calls=%async_computation.4 | async-start | bytes 131072 | tf_op jit(solution)/shard_map/psum | solution.py:207
  65.4 155.8 %all-gather.7.cloned.1.call-start = ((), (), s32[]{:S(2)}) async-start(), calls=%async_computation.2 | async-start | bytes 1179648 | tf_op jit(solution)/shard_map/all_gather | solution.py:242
  67.0 182.8 %all-reduce.3.cloned.1.call-start = ((), (), s32[]{:S(2)}) async-start(), calls=%async_computation.3 | async-start | bytes 2097152 | tf_op jit(solution)/shard_map/psum | solution.py:255
  209.6 0.8 copy-start.3
  249.8 1.2 copy-start.1
  251.0 1.2 copy-start.2
Sparse Core Ops, SparseCore 0:
  13.8 37.7 all-gather.4
  68.4 57.3 all-gather.6
Sparse Core Ops, SparseCore 1:
  69.4 140.2 all-reduce.4
  212.4 37.3 all-reduce.2

commit v2 on v1

v2 whole, which is shorter than its diff:
```python
import jax
import jax.numpy as jnp
from jax import lax
from jax.experimental import pallas as pl
from jax.experimental.pallas import tpu as pltpu
from jax.sharding import PartitionSpec as P

F32 = jnp.float32
BF16 = jnp.bfloat16
I32 = jnp.int32
I16 = jnp.int16
HIGHEST = lax.Precision.HIGHEST
MESH = pl.DeviceIdType.MESH
VMEM = pl.BlockSpec(memory_space=pltpu.VMEM)
SMEM = pl.BlockSpec(memory_space=pltpu.SMEM)
MIB = 2**20
LEVELS = 32767.0


def factor(work):
    size = work.shape[0]
    inverse = (
        lax.broadcasted_iota(I32, (size, size), 0) == lax.broadcasted_iota(I32, (size, size), 1)
    ).astype(F32)
    upper_rows, inverse_rows = [], []
    base = 0
    for j in range(size):
        start = j // 8 * 8
        if start > base:
            work, inverse, base = work[start - base :], inverse[start - base :], start
        k = j - base
        column = work[:, j : j + 1]
        pivot = column[k : k + 1]
        row, inverse_row = work[k : k + 1], inverse[k : k + 1]
        scale = 1.0 / jnp.sqrt(pivot)
        upper_rows.append(row * scale)
        inverse_rows.append(inverse_row * scale)
        if j + 1 < size:
            below = lax.broadcasted_iota(I32, (size - base, 1), 0) > k
            ratio = jnp.where(below, column * (1.0 / pivot), 0.0)
            work = work - ratio * row
            inverse = inverse - ratio * inverse_row
    return jnp.concatenate(upper_rows, axis=0), jnp.concatenate(inverse_rows, axis=0)


def factor_kernel(corner_ref, lower_ref, inverse_ref):
    upper, inverse = factor(corner_ref[...])
    size = upper.shape[0]
    keep = lax.broadcasted_iota(I32, (size, size), 0) <= lax.broadcasted_iota(
        I32, (size, size), 1
    )
    lower_ref[...] = jnp.where(keep, upper, 0.0).T
    inverse_ref[...] = inverse


def lead_factor(corner):
    shape = jax.ShapeDtypeStruct(corner.shape, F32)
    return pl.pallas_call(
        factor_kernel,
        out_shape=(shape, shape),
        in_specs=[VMEM],
        out_specs=(VMEM, VMEM),
        name="lead_factor",
        cost_estimate=pl.CostEstimate(flops=10**10, bytes_accessed=2 * 10**5, transcendentals=0),
        compiler_params=pltpu.CompilerParams(vmem_limit_bytes=16 * MIB),
    )(corner)


def greet(scen_count, link_count):
    scen, link = lax.axis_index("scen"), lax.axis_index("link")
    barrier = pltpu.get_barrier_semaphore()

    @pl.loop(1, scen_count)
    def _(step):
        pl.semaphore_signal(
            barrier,
            inc=1,
            device_id={"scen": lax.rem(scen + step, scen_count)},
            device_id_type=MESH,
        )

    for step in range(1, link_count):
        pl.semaphore_signal(
            barrier,
            inc=1,
            device_id={"link": lax.rem(link + step, link_count)},
            device_id_type=MESH,
        )
    pl.semaphore_wait(barrier, scen_count + link_count - 2)


def corner_kernel(
    scen_count,
    link_count,
    share_ref,
    pattern_ref,
    corner_ref,
    patterns_ref,
    shares_ref,
    send_sem,
    recv_sem,
    link_send,
    link_recv,
    local_sem,
):
    scen, link = lax.axis_index("scen"), lax.axis_index("link")
    greet(scen_count, link_count)

    def share_copy(source, peer):
        return pltpu.make_async_remote_copy(
            src_ref=share_ref,
            dst_ref=shares_ref.at[source],
            send_sem=send_sem.at[0, peer],
            recv_sem=recv_sem.at[0, source],
            device_id={"scen": peer},
            device_id_type=MESH,
        )

    def pattern_copy(source, peer):
        return pltpu.make_async_remote_copy(
            src_ref=pattern_ref,
            dst_ref=patterns_ref.at[source],
            send_sem=send_sem.at[1, peer],
            recv_sem=recv_sem.at[1, source],
            device_id={"scen": peer},
            device_id_type=MESH,
        )

    def corner_copy(target):
        return pltpu.make_async_remote_copy(
            src_ref=corner_ref,
            dst_ref=corner_ref,
            send_sem=link_send.at[target],
            recv_sem=link_recv,
            device_id={"link": target},
            device_id_type=MESH,
        )

    @pl.when(link == 0)
    def _():
        @pl.loop(1, scen_count)
        def _(step):
            share_copy(scen, lax.rem(scen + step, scen_count)).start()

    @pl.loop(1, scen_count)
    def _(step):
        pattern_copy(scen, lax.rem(scen + step, scen_count)).start()

    own = pltpu.make_async_copy(pattern_ref, patterns_ref.at[scen], local_sem.at[0])
    own.start()

    @pl.when(link == 0)
    def _():
        kept = pltpu.make_async_copy(share_ref, shares_ref.at[scen], local_sem.at[1])
        kept.start()
        kept.wait()

        @pl.loop(1, scen_count)
        def _(step):
            peer = lax.rem(scen + step, scen_count)
            share_copy(peer, peer).wait_recv()

        corner_ref[...] = shares_ref[0]

        @pl.loop(1, scen_count)
        def _(source):
            corner_ref[...] += shares_ref[source]

        for target in range(1, link_count):
            corner_copy(target).start()

        @pl.loop(1, scen_count)
        def _(step):
            share_copy(scen, lax.rem(scen + step, scen_count)).wait_send()

        for target in range(1, link_count):
            corner_copy(target).wait_send()

    own.wait()

    @pl.loop(1, scen_count)
    def _(step):
        peer = lax.rem(scen + step, scen_count)
        pattern_copy(peer, peer).wait()

    @pl.when(link != 0)
    def _():
        corner_copy(0).wait_recv()


def sum_corner(share, pattern, scen_count, link_count):
    tile = share.shape[0]
    dma = pltpu.SemaphoreType.DMA
    return pl.pallas_call(
        lambda *refs: corner_kernel(scen_count, link_count, *refs),
        out_shape=(
            jax.ShapeDtypeStruct((tile, tile), F32),
            jax.ShapeDtypeStruct((scen_count,) + pattern.shape, I32),
        ),
        in_specs=[VMEM, VMEM],
        out_specs=(VMEM, VMEM),
        scratch_shapes=[
            pltpu.VMEM((scen_count, tile, tile), F32),
            dma((2, scen_count)),
            dma((2, scen_count)),
            dma((link_count,)),
            dma,
            dma((2,)),
        ],
        name="sum_corner",
        cost_estimate=pl.CostEstimate(flops=8 * 10**9, bytes_accessed=10**6, transcendentals=0),
        compiler_params=pltpu.CompilerParams(
            collective_id=0, has_side_effects=True, vmem_limit_bytes=16 * MIB
        ),
    )(share, pattern)


def contribute_kernel(limit, clear, target_ref, rows_ref, own_ref, coded_ref, scales_ref):
    scenario, piece = pl.program_id(0), pl.program_id(1)
    tile = coded_ref.shape[3]
    slots = coded_ref.shape[1]
    spread = slots * pl.num_programs(1)
    if clear:

        @pl.when((scenario == 0) & (piece == 0))
        def _():
            coded_ref[...] = jnp.zeros_like(coded_ref)
            scales_ref[...] = jnp.zeros_like(scales_ref)

    product = lax.dot_general(
        rows_ref[0, 0], own_ref[0], (((0,), (0,)), ((), ())), preferred_element_type=F32
    )
    for slab in range(slots):
        values = product[slab * tile : (slab + 1) * tile]
        target = target_ref[scenario * spread + piece * slots + slab]
        dest = target // limit
        rank = target - dest * limit
        peak = jnp.max(jnp.abs(values), axis=0, keepdims=True)
        gain = jnp.where(peak > 1e-30, LEVELS / jnp.maximum(peak, 1e-30), 0.0)
        code = jnp.round(values * gain).astype(I32).astype(I16)
        scales_ref[dest, pl.ds(rank, 1), :] = peak * (1.0 / LEVELS)
        for slot in range(slots):
            coded_ref[dest, slot, pl.ds(pl.multiple_of(rank * tile, tile), tile), :] = code[
                :, slot * tile : (slot + 1) * tile
            ]


def contribute(target, gathered, own, tile, scen_count, limit):
    link_count, scen_here, depth, width = gathered.shape
    slots = width // tile
    clear = scen_count * limit > target.shape[0]
    return pl.pallas_call(
        lambda *refs: contribute_kernel(limit, clear, *refs),
        grid_spec=pltpu.PrefetchScalarGridSpec(
            num_scalar_prefetch=1,
            grid=(scen_here, link_count),
            in_specs=[
                pl.BlockSpec((1, 1, depth, width), lambda i, j, _: (j, i, 0, 0)),
                pl.BlockSpec((1, depth, width), lambda i, j, _: (i, 0, 0)),
            ],
            out_specs=[
                pl.BlockSpec((scen_count, slots, limit * tile, tile), lambda i, j, _: (0, 0, 0, 0)),
                pl.BlockSpec((scen_count, 8, width), lambda i, j, _: (0, 0, 0)),
            ],
        ),
        out_shape=(
            jax.ShapeDtypeStruct((scen_count, slots, limit * tile, tile), I16),
            jax.ShapeDtypeStruct((scen_count, 8, width), F32),
        ),
        name="contribute",
        compiler_params=pltpu.CompilerParams(vmem_limit_bytes=40 * MIB),
    )(target, gathered, own)


def exchange_kernel(
    scen_count,
    link_count,
    limit,
    weight_ref,
    coded_ref,
    scales_ref,
    arrived_ref,
    arrived_scales_ref,
    lead_ref,
    lead_scales_ref,
    column_ref,
    wide_ref,
    send_sem,
    recv_sem,
    local_sem,
    link_send,
    link_recv,
):
    scen, link = lax.axis_index("scen"), lax.axis_index("link")
    tile = coded_ref.shape[3]
    slots = coded_ref.shape[1]
    rows_own = column_ref.shape[0] // tile
    chunks = link_recv.shape[0]
    greet(scen_count, link_count)

    def parts(kind, dest):
        if kind == 0:
            return scales_ref.at[dest], arrived_scales_ref
        if kind <= slots:
            return coded_ref.at[dest, kind - 1], None
        if kind == slots + 1:
            return coded_ref.at[0, :, pl.ds(0, tile), :], lead_ref
        return scales_ref.at[0], lead_scales_ref

    def ends(kind, source, dest):
        src, into = parts(kind, dest)
        dst = arrived_ref.at[source, kind - 1] if into is None else into.at[source]
        return src, dst

    def copy(kind, source, peer):
        src, dst = ends(kind, source, peer)
        return pltpu.make_async_remote_copy(
            src_ref=src,
            dst_ref=dst,
            send_sem=send_sem.at[kind, peer],
            recv_sem=recv_sem.at[kind, source],
            device_id={"scen": peer},
            device_id_type=MESH,
        )

    def keep(kind):
        src, dst = ends(kind, scen, scen)
        return pltpu.make_async_copy(src, dst, local_sem.at[kind])

    def over_peers(act):
        @pl.loop(1, scen_count)
        def _(step):
            act(lax.rem(scen + step, scen_count))

    first, later = (0, 1), tuple(range(2, slots + 3))

    def start_first(peer):
        for kind in first:
            copy(kind, scen, peer).start()

    def start_later(peer):
        for kind in later:
            copy(kind, scen, peer).start()

    def finish_send(kinds):
        def act(peer):
            for kind in kinds:
                copy(kind, scen, peer).wait_send()

        return act

    def finish_recv(kinds):
        def act(peer):
            for kind in kinds:
                copy(kind, peer, peer).wait_recv()

        return act

    over_peers(start_first)
    for kind in first + later:
        keep(kind).start()
    over_peers(finish_send(first))
    over_peers(start_later)
    over_peers(finish_recv(first))
    for kind in first + later:
        keep(kind).wait()

    rows = column_ref.shape[0] // chunks

    def column_copy(piece, target, kind):
        at = pl.ds(piece * rows, rows)
        return pltpu.make_async_remote_copy(
            src_ref=column_ref.at[at],
            dst_ref=column_ref.at[at],
            send_sem=link_send.at[kind, piece],
            recv_sem=link_recv.at[piece],
            device_id={"link": target},
            device_id_type=MESH,
        )

    half = link_count // 2

    @pl.when(link == 0)
    def _():
        @pl.loop(0, scen_count)
        def _(source):
            for rank in range(limit):
                at = slice(rank * tile, (rank + 1) * tile)
                wide_ref[source * limit + rank] = (
                    arrived_ref[source, 0, at, :].astype(I32).astype(F32)
                    * arrived_scales_ref[source, rank : rank + 1, :tile]
                )

        per_chunk = rows_own // chunks
        for piece in range(chunks):
            for inner in range(per_chunk):
                block = piece * per_chunk + inner

                def add(listed, total, block=block):
                    return total + weight_ref[block, listed] * wide_ref[listed]

                column_ref[block * tile : (block + 1) * tile, :] = lax.fori_loop(
                    0, scen_count * limit, add, jnp.zeros((tile, tile), F32), unroll=4
                )
            column_copy(piece, half, 0).start()
            for target in range(1, half):
                column_copy(piece, target, target).start()
        for piece in range(chunks):
            for kind in range(half):
                column_copy(piece, half, kind).wait_send()

    @pl.when(link != 0)
    def _():
        for piece in range(chunks):
            column_copy(piece, 0, 0).wait_recv()

            @pl.when(link == half)
            def _():
                for target in range(half + 1, link_count):
                    column_copy(piece, target, target - half).start()

        @pl.when(link == half)
        def _():
            for piece in range(chunks):
                for kind in range(1, half):
                    column_copy(piece, half + 1, kind).wait_send()

    over_peers(finish_recv(later))
    over_peers(finish_send(later))


def exchange(weight, coded, scales, tile, limit, link_count):
    scen_count, slots = coded.shape[:2]
    rows_own = weight.shape[0]
    kinds = slots + 3
    chunks = min(4, rows_own)
    dma = pltpu.SemaphoreType.DMA
    return pl.pallas_call(
        lambda *refs: exchange_kernel(scen_count, link_count, limit, *refs),
        out_shape=(
            jax.ShapeDtypeStruct(coded.shape, I16),
            jax.ShapeDtypeStruct(scales.shape, F32),
            jax.ShapeDtypeStruct((scen_count, slots, tile, tile), I16),
            jax.ShapeDtypeStruct(scales.shape, F32),
            jax.ShapeDtypeStruct((rows_own * tile, tile), F32),
        ),
        in_specs=[SMEM, VMEM, VMEM],
        out_specs=(VMEM,) * 5,
        scratch_shapes=[
            pltpu.VMEM((scen_count * limit, tile, tile), F32),
            dma((kinds, scen_count)),
            dma((kinds, scen_count)),
            dma((kinds,)),
            dma((max(1, link_count // 2), chunks)),
            dma((chunks,)),
        ],
        name="exchange",
        compiler_params=pltpu.CompilerParams(
            collective_id=1, has_side_effects=True, vmem_limit_bytes=48 * MIB
        ),
    )(weight, coded, scales)


def split(value):
    high = value.astype(BF16)
    return high, (value - high.astype(F32)).astype(BF16)


def finish_kernel(
    limit,
    place_ref,
    row_label_ref,
    col_label_ref,
    lead_label_ref,
    arrived_ref,
    scales_ref,
    lead_ref,
    lead_scales_ref,
    column_ref,
    lower_ref,
    inverse_ref,
    diag_ref,
    panel_ref,
    trailing_ref,
    left_ref,
    raw_ref,
):
    tile = lower_ref.shape[0]
    chunk = trailing_ref.shape[1]
    slots = arrived_ref.shape[1]
    rows_own = diag_ref.shape[0]
    step = pl.program_id(0)
    per_chunk = chunk // tile
    scen, link = place_ref[0], place_ref[1]
    first_col = link * per_chunk * pl.num_programs(0)

    @pl.when(step == 0)
    def _():
        raw_ref[...] = jnp.zeros_like(raw_ref)

        @pl.loop(0, lead_ref.shape[0])
        def _(source):
            for slot in range(slots):
                at = pl.multiple_of(lead_label_ref[source * slots + slot] * tile, tile)
                raw_ref[:, pl.ds(at, tile)] += (
                    lead_ref[source, slot].astype(I32).astype(F32)
                    * lead_scales_ref[source, 0:1, slot * tile : (slot + 1) * tile]
                )

        @pl.loop(0, rows_own)
        def _(row):
            at = pl.ds(pl.multiple_of(row * tile, tile), tile)
            solved = lax.dot_general(
                column_ref[at, :],
                inverse_ref[...],
                (((1,), (1,)), ((), ())),
                precision=HIGHEST,
                preferred_element_type=F32,
            )
            mine = jnp.where((scen == 0) & (row == 0), lower_ref[...], solved)
            panel_ref[at, :] = mine
            high, low = split(-mine)
            left_ref[at, :tile] = high
            left_ref[at, tile : 2 * tile] = low
            left_ref[at, 2 * tile :] = high

    part = jnp.dot(
        inverse_ref[...],
        raw_ref[:, pl.ds(pl.multiple_of(step * chunk, chunk), chunk)],
        precision=HIGHEST,
        preferred_element_type=F32,
    )
    is_lead = (link == 0) & (step == 0)
    top = jnp.where(is_lead, lower_ref[...].T, part[:, :tile])
    part = jnp.concatenate([top, part[:, tile:]], axis=1) if per_chunk > 1 else top
    high, low = split(part)
    right = jnp.concatenate([high, high, low], axis=0)
    strip = 2 * tile if rows_own % 2 == 0 else tile
    for at in range(0, rows_own * tile, strip):
        trailing_ref[at : at + strip, :] = jnp.dot(
            left_ref[at : at + strip, :], right, preferred_element_type=F32
        )

    @pl.loop(0, arrived_ref.shape[0])
    def _(source):
        for rank in range(limit):
            row = row_label_ref[source * limit + rank]
            for slot in range(slots):
                col = col_label_ref[(source * limit + rank) * slots + slot] - step * per_chunk

                @pl.when((row >= 0) & (col >= 0) & (col < per_chunk))
                def _():
                    down = pl.ds(pl.multiple_of(row * tile, tile), tile)
                    along = pl.ds(pl.multiple_of(col * tile, tile), tile)
                    trailing_ref[down, along] += (
                        arrived_ref[source, slot, rank * tile : (rank + 1) * tile, :]
                        .astype(I32)
                        .astype(F32)
                        * scales_ref[source, rank : rank + 1, slot * tile : (slot + 1) * tile]
                    )

    unit = lax.broadcasted_iota(I32, (tile, tile), 0) == lax.broadcasted_iota(
        I32, (tile, tile), 1
    )
    for col in range(per_chunk):
        row = first_col + step * per_chunk + col - scen * rows_own

        @pl.when((row >= 0) & (row < rows_own))
        def _():
            down = pl.ds(pl.multiple_of(row * tile, tile), tile)
            trailing_ref[down, col * tile : (col + 1) * tile] += jnp.where(
                unit, diag_ref[pl.ds(row, 1), :], 0.0
            )


def finish(place, row_labels, col_labels, lead_labels, arrays, limit, width):
    lower, diag = arrays[5], arrays[7]
    tile = lower.shape[0]
    rows = diag.shape[0] * tile
    chunk = min(512, width)
    return pl.pallas_call(
        lambda *refs: finish_kernel(limit, *refs),
        grid_spec=pltpu.PrefetchScalarGridSpec(
            num_scalar_prefetch=4,
            grid=(width // chunk,),
            in_specs=[VMEM] * len(arrays),
            out_specs=[
                pl.BlockSpec((rows, tile), lambda c, *_: (0, 0)),
                pl.BlockSpec((rows, chunk), lambda c, *_: (0, c)),
            ],
            scratch_shapes=[pltpu.VMEM((rows, 3 * tile), BF16), pltpu.VMEM((tile, width), F32)],
        ),
        out_shape=(
            jax.ShapeDtypeStruct((rows, tile), F32),
            jax.ShapeDtypeStruct((rows, width), F32),
        ),
        name="finish",
        compiler_params=pltpu.CompilerParams(vmem_limit_bytes=48 * MIB),
    )(place, row_labels, col_labels, lead_labels, *arrays)


def per_device(factor_inv, coupling, first_diag, pattern):
    rows_own, tile = first_diag.shape
    scen_count = lax.axis_size("scen")
    link_count = lax.axis_size("link")
    scen_pos = lax.axis_index("scen")
    link_pos = lax.axis_index("link")
    per_link = rows_own * scen_count // link_count
    scen_here, spread = pattern.shape
    width = coupling.shape[2]
    slots = width // tile

    own = jnp.einsum("snm,smc->snc", factor_inv, coupling, preferred_element_type=F32).astype(BF16)
    gathered = lax.all_gather(own, "link", axis=0, tiled=False)

    share = lax.dot_general(
        own[0, :, :tile], own[0, :, :tile], (((0,), (0,)), ((), ())), preferred_element_type=F32
    )
    unit = jnp.eye(tile, dtype=F32)
    share = share + jnp.where(scen_pos == 0, first_diag[0][:, None] * unit, 0.0)
    padded = jnp.pad(pattern, ((0, 8 - scen_here), (0, 128 - spread)))
    corner, patterns = sum_corner(share, padded, scen_count, link_count)
    patterns = patterns[:, :scen_here, :spread]
    lower, inverse = lead_factor(corner)

    picks = scen_here * slots
    owners_here = max(1, per_link // rows_own)
    limit = max(1, (picks + owners_here - 1) // owners_here)
    listed = jnp.arange(scen_here * spread, dtype=I32)

    def targets(blocks):
        owners = blocks // rows_own
        earlier = (owners[..., :, None] == owners[..., None, :]) & (
            listed[None, :] < listed[:, None]
        )
        return owners * limit + jnp.sum(earlier.astype(I32), axis=-1)

    coded, scales = contribute(
        targets(pattern.reshape(-1)), gathered, own, tile, scen_count, limit
    )

    blocks = patterns.reshape(scen_count, scen_here * spread)
    places = scen_pos * limit + jnp.arange(limit, dtype=I32)
    hit = targets(blocks)[:, :, None] == places[None, None, :]
    row_labels = (
        jnp.sum(jnp.where(hit, blocks[:, :, None] - scen_pos * rows_own + 1, 0), axis=1) - 1
    )
    own_cols = (
        lax.dynamic_slice_in_dim(patterns, link_pos * slots, slots, 2) - link_pos * per_link
    )
    slab_cols = jnp.repeat(own_cols, spread, axis=1)
    col_labels = jnp.sum(jnp.where(hit[:, :, :, None], slab_cols[:, :, None, :], 0), axis=1)
    lead_labels = own_cols[:, 0, :]
    first_col = (col_labels[:, :, 0] == 0).reshape(-1)
    row_labels = row_labels.reshape(-1)
    weight = (
        (row_labels[None, :] == jnp.arange(rows_own, dtype=I32)[:, None]) & first_col[None, :]
    ).astype(F32)

    arrived, arrived_scales, lead, lead_scales, column = exchange(
        weight, coded, scales, tile, limit, link_count
    )
    place = jnp.stack([scen_pos, link_pos]).astype(I32)
    arrays = (
        arrived, arrived_scales, lead, lead_scales, column, lower, inverse, first_diag,
    )
    return finish(
        place, row_labels, col_labels.reshape(-1), lead_labels.reshape(-1), arrays, limit,
        per_link * tile,
    )


def solution(mesh):
    in_specs = (P("scen", None, None), P("scen", None, "link"), P("scen", None), P("scen", None))
    out_specs = (P("scen", None), P("scen", "link"))
    return jax.shard_map(
        per_device, mesh=mesh, in_specs=in_specs, out_specs=out_specs, check_vma=False
    )
```

time: 287 us -> 133 us (0.46)
  the two profiles are of different devices: /device:TPU:0 before, /device:TPU:31 now
where the time goes in v2:
time: 133 us
  Pallas kernels  104 us (78%)
  between operations  14.2 us (11%)
  matrix products  5.75 us (4%)
  local copies, waits for them, and re-layouts  4.48 us (3%)
  waiting for transfers between devices  3.83 us (3%)
    pallas_call x1, Pallas kernels, exchange(): pl.pallas_call(lambda *refs: exchange_kernel(scen_count, link_count, limi...  46.5 us
    pallas_call x1, Pallas kernels, finish(): pl.pallas_call(lambda *refs: finish_kernel(limit, *refs), grid_spec=pltpu...  24.5 us
    pallas_call x1, Pallas kernels, sum_corner(): pl.pallas_call(lambda *refs: corner_kernel(scen_count, link_count, *refs)...  18.3 us
    pallas_call x1, Pallas kernels, lead_factor(): pl.pallas_call(factor_kernel, out_shape=(shape, shape), in_specs=[VMEM],...  10.7 us
    dot_general x1, matrix products, per_device(): jnp.einsum('snm,smc->snc', factor_inv, coupling, preferred_element_type=F32)  4.41 us
    all_gather x1, waiting for transfers between devices, per_device(): gathered = lax.all_gather(own, 'link', axis=0, tiled=False)  3.81 us
    pallas_call x1, Pallas kernels, contribute(): pl.pallas_call(lambda *refs: contribute_kernel(limit, clear, *refs), grid...  3.73 us
    unnamed x10, local copies, waits for them, and re-layouts  3.36 us
  transfers between devices with their start and end apart: 1, of which 1 were waited for; matrix products, arithmetic and copies ran while one was open for 3% of the time, Pallas kernels for 22%

profile of v2, /device:TPU:31, one launch (start us, length us, event | category | flops | bytes accessed | tf_op | source)
XLA Modules:
  0.0 133.0 jit_solution(1202269184849241028)
XLA Ops:
  7.2 1.1 copy-done
  8.4 4.4 %convolution_convert_fusion.refs_2_ = bf16[2,1024,256]{2,1,0:T(8,128)(2,1)} fusion(bf16[2,1024,1024]{2,1,0:T(8,128)(2,1)} %param.4, bf16[2,1024,256]{2,1,0:T(8,128)(2,1)S(1)} %copy-done), kind=kOutput, calls=%fused_computation | convolution fusion | flops 1074266112 | bytes 6291456 | tf_op jit(solution)/shard_map/snm,smc->snc/dot_general | solution.py:613
  12.8 0.1 reshape.184
  12.9 1.3 %convolution_add_fusion.refs_0_ = f32[128,128]{1,0:T(8,128)S(1)} fusion(bf16[2,1024,256]{2,1,0:T(8,128)(2,1)} %convolution_convert_fusion.refs_2_, f32[128]{0:T(128)S(1)} %slice_bitcast_fusion.2, pred[]{:T(512)S(6)} %eq.70), kind=kOutput, calls=%fused_computation.1 | convolution fusion | flops 33619968 | bytes 328193 | tf_op jit(solution)/shard_map/dot_general | solution.py:616
  14.3 18.3 %sum_corner.1 = (f32[128,128]{1,0:T(8,128)S(1)}, s32[8,8,128]{2,1,0:T(8,128)S(1)}) custom-call(f32[128,128]{1,0:T(8,128)S(1)} %convolution_add_fusion.refs_0_, s32[8,128]{1,0:T(8,128)S(1)} %pad.4.refs_1_), custom_call_target="tpu_custom_call" | custom-call | flops 8000000000 | bytes 1000000 | tf_op jit(solution)/shard_map/sum_corner/pallas_call | solution.py:194
  32.7 0.1 copy.14
  33.0 0.1 broadcast_in_dim.56
  33.1 0.3 convert_reduce_fusion
  33.4 0.2 select_reduce_fusion.1
  33.6 0.2 select_reduce_fusion
  33.8 0.1 copy.15
  33.9 0.1 reshape_squeeze.3.refs_3_
  34.0 0.1 copy.13
  34.0 0.1 sub.36.refs_1_
  34.1 0.1 copy.17
  34.2 0.1 eq.81
  34.3 0.1 reshape.183.refs_2_
  34.5 0.2 convert_reduce_fusion.1
  34.7 10.7 %lead_factor.1 = (f32[128,128]{1,0:T(8,128)S(1)}, f32[128,128]{1,0:T(8,128)S(1)}) custom-call(f32[128,128]{1,0:T(8,128)S(1)} %get-tuple-element.21.corner_ref), custom_call_target="tpu_custom_call" | custom-call | flops 10000000000 | bytes 200000 | tf_op jit(solution)/shard_map/lead_factor/pallas_call | solution.py:58
  45.5 3.8 %all-gather.3.cloned.1.call-done = bf16[8,1024,256]{2,1,0:T(8,128)(2,1)} async-done(((bf16[2,1024,256]{2,1,0:T(8,128)(2,1)}), bf16[8,1024,256]{2,1,0:T(8,128)(2,1)}) %all-gather.3.cloned.1.call-update) | async-done | bytes 4194320 | tf_op jit(solution)/shard_map/all_gather | solution.py:614
  49.3 2.2 %copy-done.1 = bf16[8,1024,256]{2,1,0:T(8,128)(2,1)S(1)} copy-done((bf16[8,1024,256]{2,1,0:T(8,128)(2,1)S(1)}, bf16[8,1024,256]{2,1,0:T(8,128)(2,1)}, u32[]{:S(2)}) %copy-start.1) | copy-done | bytes 4194328
  51.5 3.7 %contribute.1 = (s16[8,2,256,128]{3,2,1,0:T(8,128)(2,1)S(1)}, f32[8,8,256]{2,1,0:T(8,128)S(1)}) custom-call(s32[16]{0:T(128)S(1)} %multiply_add_fusion.1.refs_0_, bf16[4,2,1024,256]{3,2,1,0:T(8,128)(2,1)S(1)} %bitcast.15, bf16[2,1024,256]{2,1,0:T(8,128)(2,1)S(1)} %copy-done.2), custom_call_target="tpu_custom_call" | custom-call | tf_op jit(solution)/shard_map/contribute/pallas_call | solution.py:252
  55.2 46.5 %exchange.1 = (s16[8,2,256,128]{3,2,1,0:T(8,128)(2,1)S(1)}, f32[8,8,256]{2,1,0:T(8,128)S(1)}, s16[8,2,128,128]{3,2,1,0:T(8,128)(2,1)S(1)}, f32[8,8,256]{2,1,0:T(8,128)S(1)}, f32[2048,128]{1,0:T(8,128)S(1)}) custom-call(f32[16,16]{1,0:T(8,128)S(1)} %fusion.1.refs_0_, s16[8,2,256,128]{3,2,1,0:T(8,128)(2,1)S(1)} %get-tuple-element.14.refs_1_, ...), custom_call_target="tpu_custom_call" | custom-call | tf_op jit(solution)/shard_map/exchange/pallas_call | solution.py:438
  101.7 24.5 %finish.1 = (f32[2048,128]{1,0:T(8,128)}, f32[2048,4096]{1,0:T(8,128)}) custom-call(s32[2]{0:T(128)S(1)} %pad_add_fusion.refs_0_, s32[16]{0:T(128)S(1)} %sub.36.refs_1_, s32[32]{0:T(128)S(1)} %reshape.183.refs_2_, s32[16]{0:T(128)S(1)} %reshape_squeeze.3.refs_3_, s16[8,2,256,128]{3,2,1,0:T(8,128)(2,1)S(1)} %get-tuple-element.16.refs_4_, ...), custom_call_target="tpu_custom_call" | custom-call | tf_op jit(solution)/shard_map/finish/pallas_call | solution.py:581
  (28 shorter events, 0.5 us)
Async XLA Ops:
  7.2 1.2 copy-start
  7.2 5.7 %copy-start.4 = (s32[2,8]{1,0:T(2,128)S(1)}, s32[2,8]{1,0:T(2,128)}, u32[]{:S(2)}) copy-start(s32[2,8]{1,0:T(2,128)} %param.7) | copy-start | bytes 196
  7.2 5.7 %copy-start.3 = (f32[16,128]{1,0:T(8,128)S(1)}, f32[16,128]{1,0:T(8,128)}, u32[]{:S(2)}) copy-start(f32[16,128]{1,0:T(8,128)} %refs_11_.1) | copy-start | bytes 24580
  7.2 42.1 %all-gather.3.cloned.1.call-start = ((), (), s32[]{:S(2)}) async-start(), calls=%async_computation | async-start | bytes 5242880 | tf_op jit(solution)/shard_map/all_gather | solution.py:614
  34.7 14.6 %copy-start.2 = (bf16[2,1024,256]{2,1,0:T(8,128)(2,1)S(1)}, bf16[2,1024,256]{2,1,0:T(8,128)(2,1)}, u32[]{:S(2)}) copy-start(bf16[2,1024,256]{2,1,0:T(8,128)(2,1)} %convolution_convert_fusion.refs_2_) | copy-start | bytes 3145732
  49.3 2.2 %copy-start.1 = (bf16[8,1024,256]{2,1,0:T(8,128)(2,1)S(1)}, bf16[8,1024,256]{2,1,0:T(8,128)(2,1)}, u32[]{:S(2)}) copy-start(bf16[8,1024,256]{2,1,0:T(8,128)(2,1)} %all-gather.3.cloned.1.call-done) | copy-start | bytes 12582916
Sparse Core Ops, SparseCore 0:
  12.9 36.2 all-gather.2

commit v3 on v2

--- a/solution.py
+++ b/solution.py
@@ -43,7 +43,7 @@
     return jnp.concatenate(upper_rows, axis=0), jnp.concatenate(inverse_rows, axis=0)
 
 
-def factor_kernel(corner_ref, lower_ref, inverse_ref):
+def factor_into(corner_ref, lower_ref, inverse_ref):
     upper, inverse = factor(corner_ref[...])
     size = upper.shape[0]
     keep = lax.broadcasted_iota(I32, (size, size), 0) <= lax.broadcasted_iota(
@@ -51,19 +51,6 @@
     )
     lower_ref[...] = jnp.where(keep, upper, 0.0).T
     inverse_ref[...] = inverse
-
-
-def lead_factor(corner):
-    shape = jax.ShapeDtypeStruct(corner.shape, F32)
-    return pl.pallas_call(
-        factor_kernel,
-        out_shape=(shape, shape),
-        in_specs=[VMEM],
-        out_specs=(VMEM, VMEM),
-        name="lead_factor",
-        cost_estimate=pl.CostEstimate(flops=10**10, bytes_accessed=2 * 10**5, transcendentals=0),
-        compiler_params=pltpu.CompilerParams(vmem_limit_bytes=16 * MIB),
-    )(corner)
 
 
 def greet(scen_count, link_count):
@@ -89,29 +76,50 @@
     pl.semaphore_wait(barrier, scen_count + link_count - 2)
 
 
-def corner_kernel(
+def gather_kernel(
     scen_count,
     link_count,
-    share_ref,
+    factor_ref,
+    coupling_ref,
+    diag_ref,
     pattern_ref,
+    gathered_ref,
     corner_ref,
     patterns_ref,
+    held_ref,
     shares_ref,
-    send_sem,
-    recv_sem,
+    held_sem,
+    scen_send,
+    scen_recv,
+    slab_send,
+    slab_recv,
     link_send,
     link_recv,
-    local_sem,
 ):
     scen, link = lax.axis_index("scen"), lax.axis_index("link")
+    scen_here, depth, width = coupling_ref.shape
+    tile = corner_ref.shape[0]
+    halves = 2
+    rows = depth // halves
+    half = link_count // 2
+    twin = link + 1 - 2 * lax.rem(link, 2)
+    across = lax.rem(link + half, link_count)
+
+    def fetch(scenario):
+        return pltpu.make_async_copy(
+            factor_ref.at[scenario], held_ref.at[scenario], held_sem.at[scenario]
+        )
+
+    for scenario in range(scen_here):
+        fetch(scenario).start()
     greet(scen_count, link_count)
 
     def share_copy(source, peer):
         return pltpu.make_async_remote_copy(
-            src_ref=share_ref,
+            src_ref=shares_ref.at[scen],
             dst_ref=shares_ref.at[source],
-            send_sem=send_sem.at[0, peer],
-            recv_sem=recv_sem.at[0, source],
+            send_sem=scen_send.at[0, peer],
+            recv_sem=scen_recv.at[0, source],
             device_id={"scen": peer},
             device_id_type=MESH,
         )
@@ -120,8 +128,8 @@
         return pltpu.make_async_remote_copy(
             src_ref=pattern_ref,
             dst_ref=patterns_ref.at[source],
-            send_sem=send_sem.at[1, peer],
-            recv_sem=recv_sem.at[1, source],
+            send_sem=scen_send.at[1, peer],
+            recv_sem=scen_recv.at[1, source],
             device_id={"scen": peer},
             device_id_type=MESH,
         )
@@ -136,30 +144,55 @@
             device_id_type=MESH,
         )
 
+    def slab_copy(way, scenario, piece, source, target):
+        at = gathered_ref.at[source, scenario, pl.ds(piece * rows, rows)]
+        return pltpu.make_async_remote_copy(
+            src_ref=at,
+            dst_ref=at,
+            send_sem=slab_send.at[way, scenario, piece],
+            recv_sem=slab_recv.at[way, scenario, piece],
+            device_id={"link": target},
+            device_id_type=MESH,
+        )
+
+    def over_peers(act):
+        @pl.loop(1, scen_count)
+        def _(step):
+            act(lax.rem(scen + step, scen_count))
+
+    for scenario in range(scen_here):
+        fetch(scenario).wait()
+        for piece in range(halves):
+            strip = rows // 2
+            for part in range(2):
+                down = slice(piece * rows + part * strip, piece * rows + (part + 1) * strip)
+                gathered_ref[link, scenario, down, :] = jnp.dot(
+                    held_ref[scenario, down, :],
+                    coupling_ref[scenario],
+                    preferred_element_type=F32,
+                ).astype(BF16)
+            slab_copy(1, scenario, piece, link, across).start()
+            slab_copy(0, scenario, piece, link, twin).start()
+        if scenario == 0:
+
+            @pl.when(link == 0)
+            def _():
+                lead = gathered_ref[0, 0, :, :tile]
+                share = lax.dot_general(
+                    lead, lead, (((0,), (0,)), ((), ())), preferred_element_type=F32
+                )
+                unit = lax.broadcasted_iota(I32, (tile, tile), 0) == lax.broadcasted_iota(
+                    I32, (tile, tile), 1
+                )
+                shares_ref[scen] = share + jnp.where(unit & (scen == 0), diag_ref[0:1, :], 0.0)
+                over_peers(lambda peer: share_copy(scen, peer).start())
+
+    patterns_ref[scen] = pattern_ref[...]
+    over_peers(lambda peer: pattern_copy(scen, peer).start())
+
     @pl.when(link == 0)
     def _():
-        @pl.loop(1, scen_count)
-        def _(step):
-            share_copy(scen, lax.rem(scen + step, scen_count)).start()
-
-    @pl.loop(1, scen_count)
-    def _(step):
-        pattern_copy(scen, lax.rem(scen + step, scen_count)).start()
-
-    own = pltpu.make_async_copy(pattern_ref, patterns_ref.at[scen], local_sem.at[0])
-    own.start()
-
-    @pl.when(link == 0)
-    def _():
-        kept = pltpu.make_async_copy(share_ref, shares_ref.at[scen], local_sem.at[1])
-        kept.start()
-        kept.wait()
-
-        @pl.loop(1, scen_count)
-        def _(step):
-            peer = lax.rem(scen + step, scen_count)
-            share_copy(peer, peer).wait_recv()
-
+        over_peers(lambda peer: share_copy(peer, peer).wait_recv())
         corner_ref[...] = shares_ref[0]
 
         @pl.loop(1, scen_count)
@@ -169,53 +202,68 @@
         for target in range(1, link_count):
             corner_copy(target).start()
 
-        @pl.loop(1, scen_count)
-        def _(step):
-            share_copy(scen, lax.rem(scen + step, scen_count)).wait_send()
-
+    pieces = [(scenario, piece) for scenario in range(scen_here) for piece in range(halves)]
+    for scenario, piece in pieces:
+        slab_copy(1, scenario, piece, across, across).wait_recv()
+        slab_copy(2, scenario, piece, across, twin).start()
+    beyond = lax.rem(twin + half, link_count)
+    for scenario, piece in pieces:
+        slab_copy(0, scenario, piece, twin, twin).wait_recv()
+        slab_copy(2, scenario, piece, beyond, twin).wait_recv()
+    for scenario, piece in pieces:
+        slab_copy(0, scenario, piece, link, twin).wait_send()
+        slab_copy(1, scenario, piece, link, across).wait_send()
+        slab_copy(2, scenario, piece, across, twin).wait_send()
+
+    @pl.when(link == 0)
+    def _():
+        over_peers(lambda peer: share_copy(scen, peer).wait_send())
         for target in range(1, link_count):
             corner_copy(target).wait_send()
 
-    own.wait()
-
-    @pl.loop(1, scen_count)
-    def _(step):
-        peer = lax.rem(scen + step, scen_count)
-        pattern_copy(peer, peer).wait()
+    def finish_pattern(peer):
+        pattern_copy(scen, peer).wait_send()
+        pattern_copy(peer, peer).wait_recv()
+
+    over_peers(finish_pattern)
 
     @pl.when(link != 0)
     def _():
         corner_copy(0).wait_recv()
 
 
-def sum_corner(share, pattern, scen_count, link_count):
-    tile = share.shape[0]
+def gather(factor_inv, coupling, diag, pattern, scen_count, link_count):
+    tile = diag.shape[1]
     dma = pltpu.SemaphoreType.DMA
+    pieces = (3, coupling.shape[0], 2)
     return pl.pallas_call(
-        lambda *refs: corner_kernel(scen_count, link_count, *refs),
+        lambda *refs: gather_kernel(scen_count, link_count, *refs),
         out_shape=(
+            jax.ShapeDtypeStruct((link_count,) + coupling.shape, BF16),
             jax.ShapeDtypeStruct((tile, tile), F32),
             jax.ShapeDtypeStruct((scen_count,) + pattern.shape, I32),
         ),
-        in_specs=[VMEM, VMEM],
-        out_specs=(VMEM, VMEM),
+        in_specs=[pl.BlockSpec(memory_space=pl.ANY), VMEM, VMEM, VMEM],
+        out_specs=(VMEM, VMEM, VMEM),
         scratch_shapes=[
+            pltpu.VMEM(factor_inv.shape, BF16),
             pltpu.VMEM((scen_count, tile, tile), F32),
+            dma((coupling.shape[0],)),
             dma((2, scen_count)),
             dma((2, scen_count)),
+            dma(pieces),
+            dma(pieces),
             dma((link_count,)),
             dma,
-            dma((2,)),
         ],
-        name="sum_corner",
-        cost_estimate=pl.CostEstimate(flops=8 * 10**9, bytes_accessed=10**6, transcendentals=0),
+        name="gather",
         compiler_params=pltpu.CompilerParams(
-            collective_id=0, has_side_effects=True, vmem_limit_bytes=16 * MIB
+            collective_id=0, has_side_effects=True, vmem_limit_bytes=40 * MIB
         ),
-    )(share, pattern)
-
-
-def contribute_kernel(limit, clear, target_ref, rows_ref, own_ref, coded_ref, scales_ref):
+    )(factor_inv, coupling, diag, pattern)
+
+
+def contribute_kernel(limit, clear, target_ref, link_ref, rows_ref, own_ref, coded_ref, scales_ref):
     scenario, piece = pl.program_id(0), pl.program_id(1)
     tile = coded_ref.shape[3]
     slots = coded_ref.shape[1]
@@ -228,7 +276,7 @@
             scales_ref[...] = jnp.zeros_like(scales_ref)
 
     product = lax.dot_general(
-        rows_ref[0, 0], own_ref[0], (((0,), (0,)), ((), ())), preferred_element_type=F32
+        rows_ref[0, 0], own_ref[0, 0], (((0,), (0,)), ((), ())), preferred_element_type=F32
     )
     for slab in range(slots):
         values = product[slab * tile : (slab + 1) * tile]
@@ -245,22 +293,22 @@
             ]
 
 
-def contribute(target, gathered, own, tile, scen_count, limit):
+def contribute(target, link, gathered, tile, scen_count, limit):
     link_count, scen_here, depth, width = gathered.shape
     slots = width // tile
     clear = scen_count * limit > target.shape[0]
     return pl.pallas_call(
         lambda *refs: contribute_kernel(limit, clear, *refs),
         grid_spec=pltpu.PrefetchScalarGridSpec(
-            num_scalar_prefetch=1,
+            num_scalar_prefetch=2,
             grid=(scen_here, link_count),
             in_specs=[
-                pl.BlockSpec((1, 1, depth, width), lambda i, j, _: (j, i, 0, 0)),
-                pl.BlockSpec((1, depth, width), lambda i, j, _: (i, 0, 0)),
+                pl.BlockSpec((1, 1, depth, width), lambda i, j, *_: (j, i, 0, 0)),
+                pl.BlockSpec((1, 1, depth, width), lambda i, j, _, link: (link[0], i, 0, 0)),
             ],
             out_specs=[
-                pl.BlockSpec((scen_count, slots, limit * tile, tile), lambda i, j, _: (0, 0, 0, 0)),
-                pl.BlockSpec((scen_count, 8, width), lambda i, j, _: (0, 0, 0)),
+                pl.BlockSpec((scen_count, slots, limit * tile, tile), lambda i, j, *_: (0, 0, 0, 0)),
+                pl.BlockSpec((scen_count, 8, width), lambda i, j, *_: (0, 0, 0)),
             ],
         ),
         out_shape=(
@@ -269,7 +317,7 @@
         ),
         name="contribute",
         compiler_params=pltpu.CompilerParams(vmem_limit_bytes=40 * MIB),
-    )(target, gathered, own)
+    )(target, link, gathered, gathered)
 
 
 def exchange_kernel(
@@ -279,15 +327,20 @@
     weight_ref,
     coded_ref,
     scales_ref,
+    corner_ref,
     arrived_ref,
     arrived_scales_ref,
     lead_ref,
     lead_scales_ref,
     column_ref,
+    lower_ref,
+    inverse_ref,
     wide_ref,
     send_sem,
     recv_sem,
     local_sem,
+    lead_send,
+    lead_recv,
     link_send,
     link_recv,
 ):
@@ -298,19 +351,10 @@
     chunks = link_recv.shape[0]
     greet(scen_count, link_count)
 
-    def parts(kind, dest):
+    def ends(kind, source, dest):
         if kind == 0:
-            return scales_ref.at[dest], arrived_scales_ref
-        if kind <= slots:
-            return coded_ref.at[dest, kind - 1], None
-        if kind == slots + 1:
-            return coded_ref.at[0, :, pl.ds(0, tile), :], lead_ref
-        return scales_ref.at[0], lead_scales_ref
-
-    def ends(kind, source, dest):
-        src, into = parts(kind, dest)
-        dst = arrived_ref.at[source, kind - 1] if into is None else into.at[source]
-        return src, dst
+            return scales_ref.at[dest], arrived_scales_ref.at[source]
+        return coded_ref.at[dest, kind - 1], arrived_ref.at[source, kind - 1]
 
     def copy(kind, source, peer):
         src, dst = ends(kind, source, peer)
@@ -332,7 +376,7 @@
         def _(step):
             act(lax.rem(scen + step, scen_count))
 
-    first, later = (0, 1), tuple(range(2, slots + 3))
+    first, later = (0, 1), tuple(range(2, slots + 1))
 
     def start_first(peer):
         for kind in first:
@@ -356,12 +400,73 @@
 
         return act
 
+    line = scen_count // 2
+    spot, side = scen // 2, lax.rem(scen, 2)
+    pair = scen + 1 - 2 * side
+
+    def lead_copies(way, block, target):
+        return [
+            pltpu.make_async_remote_copy(
+                src_ref=ref.at[block],
+                dst_ref=ref.at[block],
+                send_sem=lead_send.at[which, way, block],
+                recv_sem=lead_recv.at[which, block],
+                device_id={"scen": target},
+                device_id_type=MESH,
+            )
+            for which, ref in enumerate((lead_ref, lead_scales_ref))
+        ]
+
+    def lead_wait(block):
+        for one in lead_copies(2, block, pair):
+            one.wait_recv()
+
+    def lead_pass(block, left, right, act):
+        @pl.when(left & (spot > 0))
+        def _():
+            for one in lead_copies(0, block, lax.rem(scen + scen_count - 2, scen_count)):
+                act(one)
+
+        @pl.when(right & (spot < line - 1))
+        def _():
+            for one in lead_copies(1, block, lax.rem(scen + 2, scen_count)):
+                act(one)
+
+        for one in lead_copies(2, block, pair):
+            act(one)
+
+    def begin(one):
+        one.start()
+
+    def end(one):
+        one.wait_send()
+
+    def over_line(act, arriving):
+        @pl.loop(1, line)
+        def _(step):
+            @pl.when(spot - step >= 0)
+            def _():
+                block = scen - 2 * step
+                if arriving:
+                    lead_wait(block)
+                lead_pass(block, False, True, act)
+
+            @pl.when(spot + step < line)
+            def _():
+                block = scen + 2 * step
+                if arriving:
+                    lead_wait(block)
+                lead_pass(block, True, False, act)
+
     over_peers(start_first)
+    lead_ref[scen] = coded_ref[0, :, :tile, :]
+    lead_scales_ref[scen] = scales_ref[0]
+    lead_pass(scen, True, True, begin)
     for kind in first + later:
         keep(kind).start()
+    factor_into(corner_ref, lower_ref, inverse_ref)
     over_peers(finish_send(first))
     over_peers(start_later)
-    over_peers(finish_recv(first))
     for kind in first + later:
         keep(kind).wait()
 
@@ -382,6 +487,8 @@
 
     @pl.when(link == 0)
     def _():
+        over_peers(finish_recv(first))
+
         @pl.loop(0, scen_count)
         def _(source):
             for rank in range(limit):
@@ -405,12 +512,17 @@
             column_copy(piece, half, 0).start()
             for target in range(1, half):
                 column_copy(piece, target, target).start()
+    over_line(begin, True)
+
+    @pl.when(link == 0)
+    def _():
         for piece in range(chunks):
             for kind in range(half):
                 column_copy(piece, half, kind).wait_send()
 
     @pl.when(link != 0)
     def _():
+        over_peers(finish_recv(first))
         for piece in range(chunks):
             column_copy(piece, 0, 0).wait_recv()
 
@@ -425,14 +537,21 @@
                 for kind in range(1, half):
                     column_copy(piece, half + 1, kind).wait_send()
 
+    @pl.loop(0, line)
+    def _(step):
+        lead_wait(2 * step + 1 - side)
+
+    lead_pass(scen, True, True, end)
+    over_line(end, False)
     over_peers(finish_recv(later))
     over_peers(finish_send(later))
 
 
-def exchange(weight, coded, scales, tile, limit, link_count):
+def exchange(weight, coded, scales, corner, limit, link_count):
+    tile = corner.shape[0]
     scen_count, slots = coded.shape[:2]
     rows_own = weight.shape[0]
-    kinds = slots + 3
+    kinds = slots + 1
     chunks = min(4, rows_own)
     dma = pltpu.SemaphoreType.DMA
     return pl.pallas_call(
@@ -443,14 +562,18 @@
             jax.ShapeDtypeStruct((scen_count, slots, tile, tile), I16),
             jax.ShapeDtypeStruct(scales.shape, F32),
             jax.ShapeDtypeStruct((rows_own * tile, tile), F32),
+            jax.ShapeDtypeStruct((tile, tile), F32),
+            jax.ShapeDtypeStruct((tile, tile), F32),
         ),
-        in_specs=[SMEM, VMEM, VMEM],
-        out_specs=(VMEM,) * 5,
+        in_specs=[SMEM, VMEM, VMEM, VMEM],
+        out_specs=(VMEM,) * 7,
         scratch_shapes=[
             pltpu.VMEM((scen_count * limit, tile, tile), F32),
             dma((kinds, scen_count)),
             dma((kinds, scen_count)),
             dma((kinds,)),
+            dma((2, 3, scen_count)),
+            dma((2, scen_count)),
             dma((max(1, link_count // 2), chunks)),
             dma((chunks,)),
         ],
@@ -458,7 +581,7 @@
         compiler_params=pltpu.CompilerParams(
             collective_id=1, has_side_effects=True, vmem_limit_bytes=48 * MIB
         ),
-    )(weight, coded, scales)
+    )(weight, coded, scales, corner)
 
 
 def split(value):
@@ -484,6 +607,8 @@
     trailing_ref,
     left_ref,
     raw_ref,
+    list_ref,
+    count_ref,
 ):
     tile = lower_ref.shape[0]
     chunk = trailing_ref.shape[1]
@@ -507,9 +632,9 @@
                     * lead_scales_ref[source, 0:1, slot * tile : (slot + 1) * tile]
                 )
 
-        @pl.loop(0, rows_own)
-        def _(row):
-            at = pl.ds(pl.multiple_of(row * tile, tile), tile)
+        group = min(4, rows_own) * tile
+        for start in range(0, rows_own * tile, group):
+            at = slice(start, start + group)
             solved = lax.dot_general(
                 column_ref[at, :],
                 inverse_ref[...],
@@ -517,12 +642,26 @@
                 precision=HIGHEST,
                 preferred_element_type=F32,
             )
-            mine = jnp.where((scen == 0) & (row == 0), lower_ref[...], solved)
-            panel_ref[at, :] = mine
-            high, low = split(-mine)
+            if start == 0:
+                top = jnp.where(scen == 0, lower_ref[...], solved[:tile])
+                solved = jnp.concatenate([top, solved[tile:]], axis=0)
+            panel_ref[at, :] = solved
+            high, low = split(-solved)
             left_ref[at, :tile] = high
             left_ref[at, tile : 2 * tile] = low
             left_ref[at, 2 * tile :] = high
+
+        for other in range(count_ref.shape[0]):
+            count_ref[other] = 0
+
+        @pl.loop(0, list_ref.shape[1])
+        def _(entry):
+            @pl.when(row_label_ref[entry // slots] >= 0)
+            def _():
+                owner = col_label_ref[entry] // per_chunk
+                held = count_ref[owner]
+                list_ref[owner, held] = entry
+                count_ref[owner] = held + 1
 
     part = jnp.dot(
         inverse_ref[...],
@@ -541,23 +680,23 @@
             left_ref[at : at + strip, :], right, preferred_element_type=F32
         )
 
-    @pl.loop(0, arrived_ref.shape[0])
-    def _(source):
-        for rank in range(limit):
-            row = row_label_ref[source * limit + rank]
-            for slot in range(slots):
-                col = col_label_ref[(source * limit + rank) * slots + slot] - step * per_chunk
-
-                @pl.when((row >= 0) & (col >= 0) & (col < per_chunk))
-                def _():
-                    down = pl.ds(pl.multiple_of(row * tile, tile), tile)
-                    along = pl.ds(pl.multiple_of(col * tile, tile), tile)
-                    trailing_ref[down, along] += (
-                        arrived_ref[source, slot, rank * tile : (rank + 1) * tile, :]
-                        .astype(I32)
-                        .astype(F32)
-                        * scales_ref[source, rank : rank + 1, slot * tile : (slot + 1) * tile]
-                    )
+    @pl.loop(0, count_ref[step])
+    def _(place):
+        entry = list_ref[step, place]
+        listed = entry // slots
+        slot = entry - listed * slots
+        source = listed // limit
+        rank = listed - source * limit
+        col = col_label_ref[entry] - step * per_chunk
+        down = pl.ds(pl.multiple_of(row_label_ref[listed] * tile, tile), tile)
+        along = pl.ds(pl.multiple_of(col * tile, tile), tile)
+        from_rows = pl.ds(pl.multiple_of(rank * tile, tile), tile)
+        from_lanes = pl.ds(pl.multiple_of(slot * tile, tile), tile)
+        scales = scales_ref[source, :, from_lanes]
+        picked = lax.broadcasted_iota(I32, scales.shape, 0) == rank
+        scale = jnp.sum(jnp.where(picked, scales, 0.0), axis=0, keepdims=True)
+        codes = arrived_ref[source, slot, from_rows, :]
+        trailing_ref[down, along] += codes.astype(I32).astype(F32) * scale
 
     unit = lax.broadcasted_iota(I32, (tile, tile), 0) == lax.broadcasted_iota(
         I32, (tile, tile), 1
@@ -588,7 +727,12 @@
                 pl.BlockSpec((rows, tile), lambda c, *_: (0, 0)),
                 pl.BlockSpec((rows, chunk), lambda c, *_: (0, c)),
             ],
-            scratch_shapes=[pltpu.VMEM((rows, 3 * tile), BF16), pltpu.VMEM((tile, width), F32)],
+            scratch_shapes=[
+                pltpu.VMEM((rows, 3 * tile), BF16),
+                pltpu.VMEM((tile, width), F32),
+                pltpu.SMEM((width // chunk, col_labels.shape[0]), I32),
+                pltpu.SMEM((width // chunk,), I32),
+            ],
         ),
         out_shape=(
             jax.ShapeDtypeStruct((rows, tile), F32),
@@ -610,18 +754,11 @@
     width = coupling.shape[2]
     slots = width // tile
 
-    own = jnp.einsum("snm,smc->snc", factor_inv, coupling, preferred_element_type=F32).astype(BF16)
-    gathered = lax.all_gather(own, "link", axis=0, tiled=False)
-
-    share = lax.dot_general(
-        own[0, :, :tile], own[0, :, :tile], (((0,), (0,)), ((), ())), preferred_element_type=F32
-    )
-    unit = jnp.eye(tile, dtype=F32)
-    share = share + jnp.where(scen_pos == 0, first_diag[0][:, None] * unit, 0.0)
     padded = jnp.pad(pattern, ((0, 8 - scen_here), (0, 128 - spread)))
-    corner, patterns = sum_corner(share, padded, scen_count, link_count)
+    gathered, corner, patterns = gather(
+        factor_inv, coupling, first_diag, padded, scen_count, link_count
+    )
     patterns = patterns[:, :scen_here, :spread]
-    lower, inverse = lead_factor(corner)
 
     picks = scen_here * slots
     owners_here = max(1, per_link // rows_own)
@@ -636,7 +773,7 @@
         return owners * limit + jnp.sum(earlier.astype(I32), axis=-1)
 
     coded, scales = contribute(
-        targets(pattern.reshape(-1)), gathered, own, tile, scen_count, limit
+        targets(pattern.reshape(-1)), link_pos[None].astype(I32), gathered, tile, scen_count, limit
     )
 
     blocks = patterns.reshape(scen_count, scen_here * spread)
@@ -657,8 +794,8 @@
         (row_labels[None, :] == jnp.arange(rows_own, dtype=I32)[:, None]) & first_col[None, :]
     ).astype(F32)
 
-    arrived, arrived_scales, lead, lead_scales, column = exchange(
-        weight, coded, scales, tile, limit, link_count
+    arrived, arrived_scales, lead, lead_scales, column, lower, inverse = exchange(
+        weight, coded, scales, corner, limit, link_count
     )
     place = jnp.stack([scen_pos, link_pos]).astype(I32)
     arrays = (

time: 133 us -> 110 us (0.83)
  the two profiles are of different devices: /device:TPU:31 before, /device:TPU:0 now
where the time goes in v3:
time: 110 us
  Pallas kernels  97.1 us (88%)
  local copies, waits for them, and re-layouts  10.8 us (10%)
    pallas_call x1, Pallas kernels, exchange(): pl.pallas_call(lambda *refs: exchange_kernel(scen_count, link_count, limi...  39.7 us
    pallas_call x1, Pallas kernels, gather(): pl.pallas_call(lambda *refs: gather_kernel(scen_count, link_count, *refs)...  32.9 us
    pallas_call x1, Pallas kernels, finish(): pl.pallas_call(lambda *refs: finish_kernel(limit, *refs), grid_spec=pltpu...  20.7 us
    unnamed x12, local copies, waits for them, and re-layouts  8.3 us
    pallas_call x1, Pallas kernels, contribute(): pl.pallas_call(lambda *refs: contribute_kernel(limit, clear, *refs), grid...  3.69 us

profile of v3, /device:TPU:0, one launch (start us, length us, event | category | flops | bytes accessed | tf_op | source)
XLA Modules:
  0.0 109.6 jit_solution(5144306651913712112)
XLA Ops:
  0.7 0.8 reshape.183
  1.5 0.2 convert_reduce_fusion.1
  1.7 0.7 pad.4.refs_3_
  2.4 2.2 %copy-done.2 = bf16[2,1024,1024]{2,1,0:T(8,128)(2,1)S(1)} copy-done((bf16[2,1024,1024]{2,1,0:T(8,128)(2,1)S(1)}, bf16[2,1024,1024]{2,1,0:T(8,128)(2,1)}, u32[]{:S(2)}) %copy-start.2) | copy-done | bytes 4194328
  4.6 1.2 %copy-done.3 = bf16[2,1024,256]{2,1,0:T(8,128)(2,1)S(1)} copy-done((bf16[2,1024,256]{2,1,0:T(8,128)(2,1)S(1)}, bf16[2,1024,256]{2,1,0:T(8,128)(2,1)}, u32[]{:S(2)}) %copy-start.3) | copy-done | bytes 1048600
  5.8 0.7 copy-done.4
  6.5 32.9 %gather.1 = (bf16[4,2,1024,256]{3,2,1,0:T(8,128)(2,1)S(1)}, f32[128,128]{1,0:T(8,128)S(1)}, s32[8,8,128]{2,1,0:T(8,128)S(1)}) custom-call(bf16[2,1024,1024]{2,1,0:T(8,128)(2,1)S(1)} %copy-done.2, bf16[2,1024,256]{2,1,0:T(8,128)(2,1)S(1)} %copy-done.3, f32[16,128]{1,0:T(8,128)S(1)} %copy-done.4, s32[8,128]{1,0:T(8,128)S(1)} %pad.4.refs_3_), custom_call_target="tpu_custom_call" | custom-call | tf_op jit(solution)/shard_map/gather/pallas_call | solution.py:239
  39.4 2.0 %copy-done = bf16[4,2,1024,256]{3,2,1,0:T(8,128)(2,1)} copy-done((bf16[4,2,1024,256]{3,2,1,0:T(8,128)(2,1)}, bf16[4,2,1024,256]{3,2,1,0:T(8,128)(2,1)S(1)}, u32[]{:S(2)}) %copy-start) | copy-done | bytes 4194328
  41.4 0.1 reshape.181
  41.7 0.1 copy.13
  41.8 0.3 convert_reduce_fusion
  42.1 0.2 select_reduce_fusion.1
  42.4 0.1 copy.12
  42.4 0.1 sub.36.refs_1_
  42.6 0.1 broadcast_in_dim.55
  42.7 0.2 select_reduce_fusion
  42.9 0.1 copy.16
  43.0 0.1 eq.73
  43.1 0.1 copy.14
  43.2 0.1 reshape.182.refs_2_
  43.3 2.2 %copy-done.1 = bf16[4,2,1024,256]{3,2,1,0:T(8,128)(2,1)S(1)} copy-done((bf16[4,2,1024,256]{3,2,1,0:T(8,128)(2,1)S(1)}, bf16[4,2,1024,256]{3,2,1,0:T(8,128)(2,1)}, u32[]{:S(2)}) %copy-start.1) | copy-done | bytes 4194328
  45.5 3.7 %contribute.1 = (s16[8,2,256,128]{3,2,1,0:T(8,128)(2,1)S(1)}, f32[8,8,256]{2,1,0:T(8,128)S(1)}) custom-call(s32[16]{0:T(128)S(1)} %multiply_add_fusion.1.refs_0_, s32[1]{0:T(128)} %bitcast.1.refs_1_, bf16[4,2,1024,256]{3,2,1,0:T(8,128)(2,1)S(1)} %copy-done.1, bf16[4,2,1024,256]{3,2,1,0:T(8,128)(2,1)S(1)} %copy-done.1), custom_call_target="tpu_custom_call" | custom-call | tf_op jit(solution)/shard_map/contribute/pallas_call | solution.py:300
  49.2 39.7 %exchange.1 = (s16[8,2,256,128]{3,2,1,0:T(8,128)(2,1)S(1)}, f32[8,8,256]{2,1,0:T(8,128)S(1)}, s16[8,2,128,128]{3,2,1,0:T(8,128)(2,1)S(1)}, f32[8,8,256]{2,1,0:T(...) custom-call(f32[16,16]{1,0:T(8,128)S(1)} %fusion.1.refs_0_, ...), custom_call_target="tpu_custom_call" | custom-call | tf_op jit(solution)/shard_map/exchange/pallas_call | solution.py:557
  88.9 20.7 %finish.1 = (f32[2048,128]{1,0:T(8,128)}, f32[2048,4096]{1,0:T(8,128)}) custom-call(s32[2]{0:T(128)S(1)} %pad_add_fusion.refs_0_, s32[16]{0:T(128)S(1)} %sub.36.refs_1_, s32[32]{0:T(128)S(1)} %reshape.182.refs_2_, s32[16]{0:T(128)S(1)} %reshape_squeeze.3.refs_3_, s16[8,2,256,128]{3,2,1,0:T(8,128)(2,1)S(1)} %get-tuple-element.19.refs_4_, ...), custom_call_target="tpu_custom_call" | custom-call | tf_op jit(solution)/shard_map/finish/pallas_call | solution.py:720
  (23 shorter events, 0.4 us)
Async XLA Ops:
  2.4 2.2 %copy-start.2 = (bf16[2,1024,1024]{2,1,0:T(8,128)(2,1)S(1)}, bf16[2,1024,1024]{2,1,0:T(8,128)(2,1)}, u32[]{:S(2)}) copy-start(bf16[2,1024,1024]{2,1,0:T(8,128)(2,1)} %refs_0_.1) | copy-start | bytes 12582916
  4.6 1.2 %copy-start.3 = (bf16[2,1024,256]{2,1,0:T(8,128)(2,1)S(1)}, bf16[2,1024,256]{2,1,0:T(8,128)(2,1)}, u32[]{:S(2)}) copy-start(bf16[2,1024,256]{2,1,0:T(8,128)(2,1)} %refs_1_.1) | copy-start | bytes 3145732
  5.8 0.7 copy-start.4
  39.4 2.0 %copy-start = (bf16[4,2,1024,256]{3,2,1,0:T(8,128)(2,1)}, bf16[4,2,1024,256]{3,2,1,0:T(8,128)(2,1)S(1)}, u32[]{:S(2)}) copy-start(bf16[4,2,1024,256]{3,2,1,0:T(8,128)(2,1)S(1)} %get-tuple-element.15.refs_2_.refs_3_) | copy-start | bytes 12582916
  43.3 2.2 %copy-start.1 = (bf16[4,2,1024,256]{3,2,1,0:T(8,128)(2,1)S(1)}, bf16[4,2,1024,256]{3,2,1,0:T(8,128)(2,1)}, u32[]{:S(2)}) copy-start(bf16[4,2,1024,256]{3,2,1,0:T(8,128)(2,1)} %copy-done) | copy-start | bytes 12582916
  45.5 43.5 %copy-start.5 = (f32[16,128]{1,0:T(8,128)S(1)}, f32[16,128]{1,0:T(8,128)}, u32[]{:S(2)}) copy-start(f32[16,128]{1,0:T(8,128)} %refs_11_.1) | copy-start | bytes 24580

commit v4 on v3

--- a/solution.py
+++ b/solution.py
@@ -12,7 +12,7 @@
 HIGHEST = lax.Precision.HIGHEST
 MESH = pl.DeviceIdType.MESH
 VMEM = pl.BlockSpec(memory_space=pltpu.VMEM)
-SMEM = pl.BlockSpec(memory_space=pltpu.SMEM)
+ANY = pl.BlockSpec(memory_space=pl.ANY)
 MIB = 2**20
 LEVELS = 32767.0
 
@@ -87,8 +87,12 @@
     corner_ref,
     patterns_ref,
     held_ref,
+    columns_ref,
+    first_ref,
+    own_ref,
     shares_ref,
     held_sem,
+    kept_sem,
     scen_send,
     scen_recv,
     slab_send,
@@ -105,13 +109,22 @@
     twin = link + 1 - 2 * lax.rem(link, 2)
     across = lax.rem(link + half, link_count)
 
-    def fetch(scenario):
+    def fetch(which, scenario):
+        src, dst = ((factor_ref, held_ref), (coupling_ref, columns_ref))[which]
         return pltpu.make_async_copy(
-            factor_ref.at[scenario], held_ref.at[scenario], held_sem.at[scenario]
-        )
-
+            src.at[scenario], dst.at[scenario], held_sem.at[which, scenario]
+        )
+
+    def keep(scenario):
+        return pltpu.make_async_copy(
+            own_ref.at[scenario], gathered_ref.at[link, scenario], kept_sem.at[scenario]
+        )
+
+    first = pltpu.make_async_copy(diag_ref, first_ref, held_sem.at[2, 0])
     for scenario in range(scen_here):
-        fetch(scenario).start()
+        for which in (1, 0):
+            fetch(which, scenario).start()
+    first.start()
     greet(scen_count, link_count)
 
     def share_copy(source, peer):
@@ -145,9 +158,10 @@
         )
 
     def slab_copy(way, scenario, piece, source, target):
-        at = gathered_ref.at[source, scenario, pl.ds(piece * rows, rows)]
+        down = pl.ds(piece * rows, rows)
+        at = gathered_ref.at[source, scenario, down]
         return pltpu.make_async_remote_copy(
-            src_ref=at,
+            src_ref=at if way == 2 else own_ref.at[scenario, down],
             dst_ref=at,
             send_sem=slab_send.at[way, scenario, piece],
             recv_sem=slab_recv.at[way, scenario, piece],
@@ -161,30 +175,33 @@
             act(lax.rem(scen + step, scen_count))
 
     for scenario in range(scen_here):
-        fetch(scenario).wait()
+        fetch(1, scenario).wait()
+        fetch(0, scenario).wait()
         for piece in range(halves):
             strip = rows // 2
             for part in range(2):
                 down = slice(piece * rows + part * strip, piece * rows + (part + 1) * strip)
-                gathered_ref[link, scenario, down, :] = jnp.dot(
+                own_ref[scenario, down, :] = jnp.dot(
                     held_ref[scenario, down, :],
-                    coupling_ref[scenario],
+                    columns_ref[scenario],
                     preferred_element_type=F32,
                 ).astype(BF16)
             slab_copy(1, scenario, piece, link, across).start()
             slab_copy(0, scenario, piece, link, twin).start()
+        keep(scenario).start()
         if scenario == 0:
+            first.wait()
 
             @pl.when(link == 0)
             def _():
-                lead = gathered_ref[0, 0, :, :tile]
+                lead = own_ref[0, :, :tile]
                 share = lax.dot_general(
                     lead, lead, (((0,), (0,)), ((), ())), preferred_element_type=F32
                 )
                 unit = lax.broadcasted_iota(I32, (tile, tile), 0) == lax.broadcasted_iota(
                     I32, (tile, tile), 1
                 )
-                shares_ref[scen] = share + jnp.where(unit & (scen == 0), diag_ref[0:1, :], 0.0)
+                shares_ref[scen] = share + jnp.where(unit & (scen == 0), first_ref[0:1, :], 0.0)
                 over_peers(lambda peer: share_copy(scen, peer).start())
 
     patterns_ref[scen] = pattern_ref[...]
@@ -221,6 +238,9 @@
         for target in range(1, link_count):
             corner_copy(target).wait_send()
 
+    for scenario in range(scen_here):
+        keep(scenario).wait()
+
     def finish_pattern(peer):
         pattern_copy(scen, peer).wait_send()
         pattern_copy(peer, peer).wait_recv()
@@ -243,11 +263,15 @@
             jax.ShapeDtypeStruct((tile, tile), F32),
             jax.ShapeDtypeStruct((scen_count,) + pattern.shape, I32),
         ),
-        in_specs=[pl.BlockSpec(memory_space=pl.ANY), VMEM, VMEM, VMEM],
-        out_specs=(VMEM, VMEM, VMEM),
+        in_specs=[ANY, ANY, ANY, VMEM],
+        out_specs=(ANY, VMEM, VMEM),
         scratch_shapes=[
             pltpu.VMEM(factor_inv.shape, BF16),
+            pltpu.VMEM(coupling.shape, BF16),
+            pltpu.VMEM(diag.shape, F32),
+            pltpu.VMEM(coupling.shape, BF16),
             pltpu.VMEM((scen_count, tile, tile), F32),
+            dma((3, coupling.shape[0])),
             dma((coupling.shape[0],)),
             dma((2, scen_count)),
             dma((2, scen_count)),
@@ -258,13 +282,38 @@
         ],
         name="gather",
         compiler_params=pltpu.CompilerParams(
-            collective_id=0, has_side_effects=True, vmem_limit_bytes=40 * MIB
+            collective_id=0, has_side_effects=True, vmem_limit_bytes=60 * MIB
         ),
     )(factor_inv, coupling, diag, pattern)
 
 
-def contribute_kernel(limit, clear, target_ref, link_ref, rows_ref, own_ref, coded_ref, scales_ref):
+def contribute_kernel(
+    limit,
+    rows_own,
+    clear,
+    block_ref,
+    link_ref,
+    rows_ref,
+    own_ref,
+    coded_ref,
+    scales_ref,
+    target_ref,
+    count_ref,
+):
     scenario, piece = pl.program_id(0), pl.program_id(1)
+
+    @pl.when((scenario == 0) & (piece == 0))
+    def _():
+        @pl.loop(0, count_ref.shape[0])
+        def _(owner):
+            count_ref[owner] = 0
+
+        for listed in range(target_ref.shape[0]):
+            owner = block_ref[listed] // rows_own
+            rank = count_ref[owner]
+            target_ref[listed] = owner * limit + rank
+            count_ref[owner] = rank + 1
+
     tile = coded_ref.shape[3]
     slots = coded_ref.shape[1]
     spread = slots * pl.num_programs(1)
@@ -293,12 +342,12 @@
             ]
 
 
-def contribute(target, link, gathered, tile, scen_count, limit):
+def contribute(blocks, link, gathered, tile, scen_count, rows_own, limit):
     link_count, scen_here, depth, width = gathered.shape
     slots = width // tile
-    clear = scen_count * limit > target.shape[0]
+    clear = scen_count * limit > blocks.shape[0]
     return pl.pallas_call(
-        lambda *refs: contribute_kernel(limit, clear, *refs),
+        lambda *refs: contribute_kernel(limit, rows_own, clear, *refs),
         grid_spec=pltpu.PrefetchScalarGridSpec(
             num_scalar_prefetch=2,
             grid=(scen_here, link_count),
@@ -310,21 +359,23 @@
                 pl.BlockSpec((scen_count, slots, limit * tile, tile), lambda i, j, *_: (0, 0, 0, 0)),
                 pl.BlockSpec((scen_count, 8, width), lambda i, j, *_: (0, 0, 0)),
             ],
+            scratch_shapes=[
+                pltpu.SMEM((blocks.shape[0],), I32),
+                pltpu.SMEM((scen_count,), I32),
+            ],
         ),
         out_shape=(
             jax.ShapeDtypeStruct((scen_count, slots, limit * tile, tile), I16),
             jax.ShapeDtypeStruct((scen_count, 8, width), F32),
         ),
         name="contribute",
-        compiler_params=pltpu.CompilerParams(vmem_limit_bytes=40 * MIB),
-    )(target, link, gathered, gathered)
+        compiler_params=pltpu.CompilerParams(vmem_limit_bytes=61 * MIB),
+    )(blocks, link, gathered, gathered)
 
 
 def exchange_kernel(
     scen_count,
     link_count,
-    limit,
-    weight_ref,
     coded_ref,
     scales_ref,
     corner_ref,
@@ -333,9 +384,9 @@
     lead_ref,
     lead_scales_ref,
     column_ref,
+    column_scales_ref,
     lower_ref,
     inverse_ref,
-    wide_ref,
     send_sem,
     recv_sem,
     local_sem,
@@ -347,8 +398,6 @@
     scen, link = lax.axis_index("scen"), lax.axis_index("link")
     tile = coded_ref.shape[3]
     slots = coded_ref.shape[1]
-    rows_own = column_ref.shape[0] // tile
-    chunks = link_recv.shape[0]
     greet(scen_count, link_count)
 
     def ends(kind, source, dest):
@@ -470,72 +519,79 @@
     for kind in first + later:
         keep(kind).wait()
 
-    rows = column_ref.shape[0] // chunks
-
-    def column_copy(piece, target, kind):
-        at = pl.ds(piece * rows, rows)
-        return pltpu.make_async_remote_copy(
-            src_ref=column_ref.at[at],
-            dst_ref=column_ref.at[at],
-            send_sem=link_send.at[kind, piece],
-            recv_sem=link_recv.at[piece],
-            device_id={"link": target},
-            device_id_type=MESH,
-        )
-
     half = link_count // 2
+
+    def column_copies(source, target, way, relayed):
+        pairs = (
+            (column_ref if relayed else arrived_ref.at[:, 0], column_ref),
+            (column_scales_ref if relayed else arrived_scales_ref, column_scales_ref),
+        )
+        return [
+            pltpu.make_async_remote_copy(
+                src_ref=src.at[source],
+                dst_ref=dst.at[source],
+                send_sem=link_send.at[which, way, source],
+                recv_sem=link_recv.at[which, source],
+                device_id={"link": target},
+                device_id_type=MESH,
+            )
+            for which, (src, dst) in enumerate(pairs)
+        ]
+
+    def column_out(source):
+        for target in (half,) + tuple(range(1, half)):
+            for one in column_copies(source, target, target % half, False):
+                one.start()
+
+    def column_out_end(source):
+        for target in (half,) + tuple(range(1, half)):
+            for one in column_copies(source, target, target % half, False):
+                one.wait_send()
 
     @pl.when(link == 0)
     def _():
-        over_peers(finish_recv(first))
+        column_out(scen)
+
+        @pl.loop(1, scen_count)
+        def _(step):
+            peer = lax.rem(scen + step, scen_count)
+            finish_recv(first)(peer)
+            column_out(peer)
+
+    over_line(begin, True)
+
+    @pl.when(link == 0)
+    def _():
+        column_ref[...] = arrived_ref[:, 0]
+        column_scales_ref[...] = arrived_scales_ref[...]
 
         @pl.loop(0, scen_count)
         def _(source):
-            for rank in range(limit):
-                at = slice(rank * tile, (rank + 1) * tile)
-                wide_ref[source * limit + rank] = (
-                    arrived_ref[source, 0, at, :].astype(I32).astype(F32)
-                    * arrived_scales_ref[source, rank : rank + 1, :tile]
-                )
-
-        per_chunk = rows_own // chunks
-        for piece in range(chunks):
-            for inner in range(per_chunk):
-                block = piece * per_chunk + inner
-
-                def add(listed, total, block=block):
-                    return total + weight_ref[block, listed] * wide_ref[listed]
-
-                column_ref[block * tile : (block + 1) * tile, :] = lax.fori_loop(
-                    0, scen_count * limit, add, jnp.zeros((tile, tile), F32), unroll=4
-                )
-            column_copy(piece, half, 0).start()
-            for target in range(1, half):
-                column_copy(piece, target, target).start()
-    over_line(begin, True)
-
-    @pl.when(link == 0)
-    def _():
-        for piece in range(chunks):
-            for kind in range(half):
-                column_copy(piece, half, kind).wait_send()
+            column_out_end(source)
 
     @pl.when(link != 0)
     def _():
         over_peers(finish_recv(first))
-        for piece in range(chunks):
-            column_copy(piece, 0, 0).wait_recv()
+
+        @pl.loop(0, scen_count)
+        def _(step):
+            source = lax.rem(scen + step, scen_count)
+            for one in column_copies(source, 0, 0, True):
+                one.wait_recv()
 
             @pl.when(link == half)
             def _():
                 for target in range(half + 1, link_count):
-                    column_copy(piece, target, target - half).start()
+                    for one in column_copies(source, target, target - half, True):
+                        one.start()
 
         @pl.when(link == half)
         def _():
-            for piece in range(chunks):
-                for kind in range(1, half):
-                    column_copy(piece, half + 1, kind).wait_send()
+            @pl.loop(0, scen_count)
+            def _(source):
+                for target in range(half + 1, link_count):
+                    for one in column_copies(source, target, target - half, True):
+                        one.wait_send()
 
     @pl.loop(0, line)
     def _(step):
@@ -547,41 +603,39 @@
     over_peers(finish_send(later))
 
 
-def exchange(weight, coded, scales, corner, limit, link_count):
+def exchange(coded, scales, corner, link_count):
     tile = corner.shape[0]
-    scen_count, slots = coded.shape[:2]
-    rows_own = weight.shape[0]
+    scen_count, slots, rows = coded.shape[:3]
     kinds = slots + 1
-    chunks = min(4, rows_own)
     dma = pltpu.SemaphoreType.DMA
     return pl.pallas_call(
-        lambda *refs: exchange_kernel(scen_count, link_count, limit, *refs),
+        lambda *refs: exchange_kernel(scen_count, link_count, *refs),
         out_shape=(
             jax.ShapeDtypeStruct(coded.shape, I16),
             jax.ShapeDtypeStruct(scales.shape, F32),
             jax.ShapeDtypeStruct((scen_count, slots, tile, tile), I16),
             jax.ShapeDtypeStruct(scales.shape, F32),
-            jax.ShapeDtypeStruct((rows_own * tile, tile), F32),
+            jax.ShapeDtypeStruct((scen_count, rows, tile), I16),
+            jax.ShapeDtypeStruct(scales.shape, F32),
             jax.ShapeDtypeStruct((tile, tile), F32),
             jax.ShapeDtypeStruct((tile, tile), F32),
         ),
-        in_specs=[SMEM, VMEM, VMEM, VMEM],
-        out_specs=(VMEM,) * 7,
+        in_specs=[VMEM, VMEM, VMEM],
+        out_specs=(VMEM,) * 8,
         scratch_shapes=[
-            pltpu.VMEM((scen_count * limit, tile, tile), F32),
             dma((kinds, scen_count)),
             dma((kinds, scen_count)),
             dma((kinds,)),
             dma((2, 3, scen_count)),
             dma((2, scen_count)),
-            dma((max(1, link_count // 2), chunks)),
-            dma((chunks,)),
+            dma((2, max(1, link_count // 2), scen_count)),
+            dma((2, scen_count)),
         ],
         name="exchange",
         compiler_params=pltpu.CompilerParams(
             collective_id=1, has_side_effects=True, vmem_limit_bytes=48 * MIB
         ),
-    )(weight, coded, scales, corner)
+    )(coded, scales, corner)
 
 
 def split(value):
@@ -591,15 +645,15 @@
 
 def finish_kernel(
     limit,
+    spread,
     place_ref,
-    row_label_ref,
-    col_label_ref,
-    lead_label_ref,
+    block_ref,
     arrived_ref,
     scales_ref,
     lead_ref,
     lead_scales_ref,
     column_ref,
+    column_scales_ref,
     lower_ref,
     inverse_ref,
     diag_ref,
@@ -607,7 +661,10 @@
     trailing_ref,
     left_ref,
     raw_ref,
+    sums_ref,
     list_ref,
+    row_ref,
+    col_ref,
     count_ref,
 ):
     tile = lower_ref.shape[0]
@@ -616,6 +673,7 @@
     rows_own = diag_ref.shape[0]
     step = pl.program_id(0)
     per_chunk = chunk // tile
+    listed_count = block_ref.shape[0] // lead_ref.shape[0]
     scen, link = place_ref[0], place_ref[1]
     first_col = link * per_chunk * pl.num_programs(0)
 
@@ -626,17 +684,54 @@
         @pl.loop(0, lead_ref.shape[0])
         def _(source):
             for slot in range(slots):
-                at = pl.multiple_of(lead_label_ref[source * slots + slot] * tile, tile)
+                block = block_ref[source * listed_count + link * slots + slot] - first_col
+                at = pl.multiple_of(block * tile, tile)
                 raw_ref[:, pl.ds(at, tile)] += (
                     lead_ref[source, slot].astype(I32).astype(F32)
                     * lead_scales_ref[source, 0:1, slot * tile : (slot + 1) * tile]
                 )
 
+        sums_ref[...] = jnp.zeros_like(sums_ref)
+        for other in range(count_ref.shape[0]):
+            count_ref[other] = 0
+
+        @pl.loop(0, lead_ref.shape[0])
+        def _(source):
+            def visit(listed, rank):
+                row = block_ref[source * listed_count + listed] - scen * rows_own
+                mine = (row >= 0) & (row < rows_own)
+                scenario = source * listed_count + listed // spread * spread
+
+                @pl.when(mine)
+                def _():
+                    for slot in range(slots):
+                        col = block_ref[scenario + link * slots + slot] - first_col
+                        entry = (source * limit + rank) * slots + slot
+                        owner = col // per_chunk
+                        held = count_ref[owner]
+                        list_ref[owner, held] = entry
+                        count_ref[owner] = held + 1
+                        row_ref[entry] = row
+                        col_ref[entry] = col
+
+                @pl.when(mine & (block_ref[scenario] == 0))
+                def _():
+                    scales = column_scales_ref[source, :, :tile]
+                    picked = lax.broadcasted_iota(I32, scales.shape, 0) == rank
+                    scale = jnp.sum(jnp.where(picked, scales, 0.0), axis=0, keepdims=True)
+                    codes = column_ref[source, pl.ds(pl.multiple_of(rank * tile, tile), tile), :]
+                    down = pl.ds(pl.multiple_of(row * tile, tile), tile)
+                    sums_ref[down, :] += codes.astype(I32).astype(F32) * scale
+
+                return rank + mine.astype(I32)
+
+            lax.fori_loop(0, listed_count, visit, jnp.int32(0))
+
         group = min(4, rows_own) * tile
         for start in range(0, rows_own * tile, group):
             at = slice(start, start + group)
             solved = lax.dot_general(
-                column_ref[at, :],
+                sums_ref[at, :],
                 inverse_ref[...],
                 (((1,), (1,)), ((), ())),
                 precision=HIGHEST,
@@ -651,18 +746,6 @@
             left_ref[at, tile : 2 * tile] = low
             left_ref[at, 2 * tile :] = high
 
-        for other in range(count_ref.shape[0]):
-            count_ref[other] = 0
-
-        @pl.loop(0, list_ref.shape[1])
-        def _(entry):
-            @pl.when(row_label_ref[entry // slots] >= 0)
-            def _():
-                owner = col_label_ref[entry] // per_chunk
-                held = count_ref[owner]
-                list_ref[owner, held] = entry
-                count_ref[owner] = held + 1
-
     part = jnp.dot(
         inverse_ref[...],
         raw_ref[:, pl.ds(pl.multiple_of(step * chunk, chunk), chunk)],
@@ -674,7 +757,7 @@
     part = jnp.concatenate([top, part[:, tile:]], axis=1) if per_chunk > 1 else top
     high, low = split(part)
     right = jnp.concatenate([high, high, low], axis=0)
-    strip = 2 * tile if rows_own % 2 == 0 else tile
+    strip = min(8, rows_own) * tile
     for at in range(0, rows_own * tile, strip):
         trailing_ref[at : at + strip, :] = jnp.dot(
             left_ref[at : at + strip, :], right, preferred_element_type=F32
@@ -687,8 +770,8 @@
         slot = entry - listed * slots
         source = listed // limit
         rank = listed - source * limit
-        col = col_label_ref[entry] - step * per_chunk
-        down = pl.ds(pl.multiple_of(row_label_ref[listed] * tile, tile), tile)
+        col = col_ref[entry] - step * per_chunk
+        down = pl.ds(pl.multiple_of(row_ref[entry] * tile, tile), tile)
         along = pl.ds(pl.multiple_of(col * tile, tile), tile)
         from_rows = pl.ds(pl.multiple_of(rank * tile, tile), tile)
         from_lanes = pl.ds(pl.multiple_of(slot * tile, tile), tile)
@@ -712,15 +795,16 @@
             )
 
 
-def finish(place, row_labels, col_labels, lead_labels, arrays, limit, width):
-    lower, diag = arrays[5], arrays[7]
+def finish(place, blocks, arrays, spread, limit, width):
+    lower, diag = arrays[6], arrays[8]
+    entries = arrays[0].shape[0] * arrays[0].shape[1] * limit
     tile = lower.shape[0]
     rows = diag.shape[0] * tile
     chunk = min(512, width)
     return pl.pallas_call(
-        lambda *refs: finish_kernel(limit, *refs),
+        lambda *refs: finish_kernel(limit, spread, *refs),
         grid_spec=pltpu.PrefetchScalarGridSpec(
-            num_scalar_prefetch=4,
+            num_scalar_prefetch=2,
             grid=(width // chunk,),
             in_specs=[VMEM] * len(arrays),
             out_specs=[
@@ -730,7 +814,10 @@
             scratch_shapes=[
                 pltpu.VMEM((rows, 3 * tile), BF16),
                 pltpu.VMEM((tile, width), F32),
-                pltpu.SMEM((width // chunk, col_labels.shape[0]), I32),
+                pltpu.VMEM((rows, tile), F32),
+                pltpu.SMEM((width // chunk, entries), I32),
+                pltpu.SMEM((entries,), I32),
+                pltpu.SMEM((entries,), I32),
                 pltpu.SMEM((width // chunk,), I32),
             ],
         ),
@@ -740,7 +827,7 @@
         ),
         name="finish",
         compiler_params=pltpu.CompilerParams(vmem_limit_bytes=48 * MIB),
-    )(place, row_labels, col_labels, lead_labels, *arrays)
+    )(place, blocks, *arrays)
 
 
 def per_device(factor_inv, coupling, first_diag, pattern):
@@ -763,48 +850,18 @@
     picks = scen_here * slots
     owners_here = max(1, per_link // rows_own)
     limit = max(1, (picks + owners_here - 1) // owners_here)
-    listed = jnp.arange(scen_here * spread, dtype=I32)
-
-    def targets(blocks):
-        owners = blocks // rows_own
-        earlier = (owners[..., :, None] == owners[..., None, :]) & (
-            listed[None, :] < listed[:, None]
-        )
-        return owners * limit + jnp.sum(earlier.astype(I32), axis=-1)
-
     coded, scales = contribute(
-        targets(pattern.reshape(-1)), link_pos[None].astype(I32), gathered, tile, scen_count, limit
+        pattern.reshape(-1),
+        link_pos[None].astype(I32),
+        gathered,
+        tile,
+        scen_count,
+        rows_own,
+        limit,
     )
-
-    blocks = patterns.reshape(scen_count, scen_here * spread)
-    places = scen_pos * limit + jnp.arange(limit, dtype=I32)
-    hit = targets(blocks)[:, :, None] == places[None, None, :]
-    row_labels = (
-        jnp.sum(jnp.where(hit, blocks[:, :, None] - scen_pos * rows_own + 1, 0), axis=1) - 1
-    )
-    own_cols = (
-        lax.dynamic_slice_in_dim(patterns, link_pos * slots, slots, 2) - link_pos * per_link
-    )
-    slab_cols = jnp.repeat(own_cols, spread, axis=1)
-    col_labels = jnp.sum(jnp.where(hit[:, :, :, None], slab_cols[:, :, None, :], 0), axis=1)
-    lead_labels = own_cols[:, 0, :]
-    first_col = (col_labels[:, :, 0] == 0).reshape(-1)
-    row_labels = row_labels.reshape(-1)
-    weight = (
-        (row_labels[None, :] == jnp.arange(rows_own, dtype=I32)[:, None]) & first_col[None, :]
-    ).astype(F32)
-
-    arrived, arrived_scales, lead, lead_scales, column, lower, inverse = exchange(
-        weight, coded, scales, corner, limit, link_count
-    )
+    arrays = exchange(coded, scales, corner, link_count) + (first_diag,)
     place = jnp.stack([scen_pos, link_pos]).astype(I32)
-    arrays = (
-        arrived, arrived_scales, lead, lead_scales, column, lower, inverse, first_diag,
-    )
-    return finish(
-        place, row_labels, col_labels.reshape(-1), lead_labels.reshape(-1), arrays, limit,
-        per_link * tile,
-    )
+    return finish(place, patterns.reshape(-1), arrays, spread, limit, per_link * tile)
 
 
 def solution(mesh):

time: 110 us -> 114 us (1.036)
  Pallas kernels: 97.1 us -> 108 us
  local copies, waits for them, and re-layouts: 10.8 us -> 5.53 us
    pallas_call x3, Pallas kernels: 64.2 us -> 73.3 us  [the longest x1 39.1 us: exchange(): pl.pallas_call(lambda *refs: exchange_kernel(scen_count, link_count, *ref...]
    unnamed x12 -> x8, local copies, waits for them, and re-layouts: 8.3 us -> 2.07 us
    pallas_call x1, Pallas kernels: 32.9 us -> 34.4 us  [gather(): pl.pallas_call(lambda *refs: gather_kernel(scen_count, link_count, *refs)...]
where the time goes in v4:
time: 114 us
  Pallas kernels  108 us (95%)
  local copies, waits for them, and re-layouts  5.53 us (5%)
    pallas_call x1, Pallas kernels, exchange(): pl.pallas_call(lambda *refs: exchange_kernel(scen_count, link_count, *ref...  39.1 us
    pallas_call x1, Pallas kernels, gather(): pl.pallas_call(lambda *refs: gather_kernel(scen_count, link_count, *refs)...  34.4 us
    pallas_call x1, Pallas kernels, finish(): pl.pallas_call(lambda *refs: finish_kernel(limit, spread, *refs), grid_sp...  25.8 us
    pallas_call x1, Pallas kernels, contribute(): pl.pallas_call(lambda *refs: contribute_kernel(limit, rows_own, clear, *r...  8.45 us

profile of v4, /device:TPU:0, one launch (start us, length us, event | category | flops | bytes accessed | tf_op | source)
XLA Modules:
  0.0 114.1 jit_solution(15136929559352854776)
XLA Ops:
  0.6 0.1 pad_add_fusion.refs_0_
  0.7 1.3 %reshape.11.refs_0_ = s32[16]{0:T(128)} reshape(s32[2,8]{1,0:T(2,128)} %param.7) | data formatting | bytes 128 | tf_op jit(solution)/shard_map/reshape | solution.py:854
  2.0 1.3 %pad.4.refs_3_ = s32[8,128]{1,0:T(8,128)} pad(s32[2,8]{1,0:T(2,128)} %param.7, s32[]{:T(128)} %constant.10.clone.1), padding=0_6x0_120 | pad | bytes 4164 | tf_op jit(solution)/shard_map/jit(_pad)/pad | solution.py:844
  3.3 34.4 %gather.1 = (bf16[4,2,1024,256]{3,2,1,0:T(8,128)(2,1)}, f32[128,128]{1,0:T(8,128)}, s32[8,8,128]{2,1,0:T(8,128)}) custom-call(bf16[2,1024,1024]{2,1,0:T(8,128)(2,1)} %refs_0_.1, bf16[2,1024,256]{2,1,0:T(8,128)(2,1)} %refs_1_.1, f32[16,128]{1,0:T(8,128)} %refs_10_.1, s32[8,128]{1,0:T(8,128)} %pad.4.refs_3_), custom_call_target="tpu_custom_call" | custom-call | tf_op jit(solution)/shard_map/gather/pallas_call | solution.py:259
  37.8 0.8 slice.3
  38.5 0.1 reshape.10.refs_1_
  38.6 0.0 copy-start.1
  38.6 0.0 copy-start.3
  38.7 8.4 %contribute.1 = (s16[8,2,256,128]{3,2,1,0:T(8,128)(2,1)}, f32[8,8,256]{2,1,0:T(8,128)}) custom-call(s32[16]{0:T(128)} %reshape.11.refs_0_, s32[1]{0:T(128)} %bitcast.1.refs_1_, bf16[4,2,1024,256]{3,2,1,0:T(8,128)(2,1)} %get-tuple-element.16.refs_2_.refs_3_, bf16[4,2,1024,256]{3,2,1,0:T(8,128)(2,1)} %get-tuple-element.16.refs_2_.refs_3_), custom_call_target="tpu_custom_call" | custom-call | tf_op jit(solution)/shard_map/contribute/pallas_call | solution.py:349
  47.1 0.0 copy-done.1
  47.1 0.0 copy-start
  47.1 1.2 %copy-done = s16[8,2,256,128]{3,2,1,0:T(8,128)(2,1)S(1)} copy-done((s16[8,2,256,128]{3,2,1,0:T(8,128)(2,1)S(1)}, s16[8,2,256,128]{3,2,1,0:T(8,128)(2,1)}, u32[]{:S(2)}) %copy-start) | copy-done | bytes 1048600
  48.3 0.0 copy-start.2
  48.3 0.8 copy-done.2
  49.2 39.1 %exchange.1 = (s16[8,2,256,128]{3,2,1,0:T(8,128)(2,1)S(1)}, f32[8,8,256]{2,1,0:T(8,128)S(1)}, s16[8,2,128,128]{3,2,1,0:T(8,128)(2,1)S(1)}, f32[8,8,256]{2,1,0:T(...) custom-call(s16[8,2,256,128]{3,2,1,0:T(8,128)(2,1)S(1)} %copy-done, ...), custom_call_target="tpu_custom_call" | custom-call | tf_op jit(solution)/shard_map/exchange/pallas_call | solution.py:611
  88.3 0.0 copy-done.3
  88.3 25.8 %finish.1 = (f32[2048,128]{1,0:T(8,128)}, f32[2048,4096]{1,0:T(8,128)}) custom-call(s32[2]{0:T(128)S(1)} %pad_add_fusion.refs_0_, s32[128]{0:T(128)S(1)} %reshape.10.refs_1_, s16[8,2,256,128]{3,2,1,0:T(8,128)(2,1)S(1)} %get-tuple-element.20.refs_2_, f32[8,8,256]{2,1,0:T(8,128)S(1)} %get-tuple-element.21.refs_3_, ...), custom_call_target="tpu_custom_call" | custom-call | tf_op jit(solution)/shard_map/finish/pallas_call | solution.py:804
Async XLA Ops:
  38.6 8.5 %copy-start.1 = (f32[128,128]{1,0:T(8,128)S(1)}, f32[128,128]{1,0:T(8,128)}, u32[]{:S(2)}) copy-start(f32[128,128]{1,0:T(8,128)} %get-tuple-element.19.refs_2_) | copy-start | bytes 196612
  38.6 49.6 %copy-start.3 = (f32[16,128]{1,0:T(8,128)S(1)}, f32[16,128]{1,0:T(8,128)}, u32[]{:S(2)}) copy-start(f32[16,128]{1,0:T(8,128)} %refs_10_.1) | copy-start | bytes 24580
  47.1 1.2 %copy-start = (s16[8,2,256,128]{3,2,1,0:T(8,128)(2,1)S(1)}, s16[8,2,256,128]{3,2,1,0:T(8,128)(2,1)}, u32[]{:S(2)}) copy-start(s16[8,2,256,128]{3,2,1,0:T(8,128)(2,1)} %get-tuple-element.17.refs_0_) | copy-start | bytes 3145732
  48.3 0.8 copy-start.2

commit v5 on v4

--- a/solution.py
+++ b/solution.py
@@ -288,32 +288,9 @@
 
 
 def contribute_kernel(
-    limit,
-    rows_own,
-    clear,
-    block_ref,
-    link_ref,
-    rows_ref,
-    own_ref,
-    coded_ref,
-    scales_ref,
-    target_ref,
-    count_ref,
+    limit, clear, target_ref, link_ref, rows_ref, own_ref, coded_ref, scales_ref
 ):
     scenario, piece = pl.program_id(0), pl.program_id(1)
-
-    @pl.when((scenario == 0) & (piece == 0))
-    def _():
-        @pl.loop(0, count_ref.shape[0])
-        def _(owner):
-            count_ref[owner] = 0
-
-        for listed in range(target_ref.shape[0]):
-            owner = block_ref[listed] // rows_own
-            rank = count_ref[owner]
-            target_ref[listed] = owner * limit + rank
-            count_ref[owner] = rank + 1
-
     tile = coded_ref.shape[3]
     slots = coded_ref.shape[1]
     spread = slots * pl.num_programs(1)
@@ -342,12 +319,12 @@
             ]
 
 
-def contribute(blocks, link, gathered, tile, scen_count, rows_own, limit):
+def contribute(target, link, gathered, tile, scen_count, limit):
     link_count, scen_here, depth, width = gathered.shape
     slots = width // tile
-    clear = scen_count * limit > blocks.shape[0]
+    clear = scen_count * limit > target.shape[0]
     return pl.pallas_call(
-        lambda *refs: contribute_kernel(limit, rows_own, clear, *refs),
+        lambda *refs: contribute_kernel(limit, clear, *refs),
         grid_spec=pltpu.PrefetchScalarGridSpec(
             num_scalar_prefetch=2,
             grid=(scen_here, link_count),
@@ -359,18 +336,14 @@
                 pl.BlockSpec((scen_count, slots, limit * tile, tile), lambda i, j, *_: (0, 0, 0, 0)),
                 pl.BlockSpec((scen_count, 8, width), lambda i, j, *_: (0, 0, 0)),
             ],
-            scratch_shapes=[
-                pltpu.SMEM((blocks.shape[0],), I32),
-                pltpu.SMEM((scen_count,), I32),
-            ],
         ),
         out_shape=(
             jax.ShapeDtypeStruct((scen_count, slots, limit * tile, tile), I16),
             jax.ShapeDtypeStruct((scen_count, 8, width), F32),
         ),
         name="contribute",
-        compiler_params=pltpu.CompilerParams(vmem_limit_bytes=61 * MIB),
-    )(blocks, link, gathered, gathered)
+        compiler_params=pltpu.CompilerParams(vmem_limit_bytes=32 * MIB),
+    )(target, link, gathered, gathered)
 
 
 def exchange_kernel(
@@ -381,12 +354,14 @@
     corner_ref,
     arrived_ref,
     arrived_scales_ref,
+    lower_ref,
+    side_ref,
+    down_ref,
+    inverse_ref,
     lead_ref,
     lead_scales_ref,
     column_ref,
     column_scales_ref,
-    lower_ref,
-    inverse_ref,
     send_sem,
     recv_sem,
     local_sem,
@@ -597,6 +572,27 @@
     def _(step):
         lead_wait(2 * step + 1 - side)
 
+    @pl.loop(0, scen_count)
+    def _(source):
+        for slot in range(slots):
+            at = slice(slot * tile, (slot + 1) * tile)
+            side_ref[source, slot] = jnp.dot(
+                inverse_ref[...],
+                lead_ref[source, slot].astype(I32).astype(F32) * lead_scales_ref[source, 0:1, at],
+                precision=HIGHEST,
+                preferred_element_type=F32,
+            )
+        for rank in range(column_ref.shape[1] // tile):
+            at = slice(rank * tile, (rank + 1) * tile)
+            codes = column_ref[source, at, :].astype(I32).astype(F32)
+            down_ref[source, at, :] = lax.dot_general(
+                codes * column_scales_ref[source, rank : rank + 1, :tile],
+                inverse_ref[...],
+                (((1,), (1,)), ((), ())),
+                precision=HIGHEST,
+                preferred_element_type=F32,
+            )
+
     lead_pass(scen, True, True, end)
     over_line(end, False)
     over_peers(finish_recv(later))
@@ -613,16 +609,18 @@
         out_shape=(
             jax.ShapeDtypeStruct(coded.shape, I16),
             jax.ShapeDtypeStruct(scales.shape, F32),
-            jax.ShapeDtypeStruct((scen_count, slots, tile, tile), I16),
-            jax.ShapeDtypeStruct(scales.shape, F32),
-            jax.ShapeDtypeStruct((scen_count, rows, tile), I16),
-            jax.ShapeDtypeStruct(scales.shape, F32),
             jax.ShapeDtypeStruct((tile, tile), F32),
-            jax.ShapeDtypeStruct((tile, tile), F32),
+            jax.ShapeDtypeStruct((scen_count, slots, tile, tile), F32),
+            jax.ShapeDtypeStruct((scen_count, rows, tile), F32),
         ),
         in_specs=[VMEM, VMEM, VMEM],
-        out_specs=(VMEM,) * 8,
+        out_specs=(VMEM,) * 5,
         scratch_shapes=[
+            pltpu.VMEM((tile, tile), F32),
+            pltpu.VMEM((scen_count, slots, tile, tile), I16),
+            pltpu.VMEM(scales.shape, F32),
+            pltpu.VMEM((scen_count, rows, tile), I16),
+            pltpu.VMEM(scales.shape, F32),
             dma((kinds, scen_count)),
             dma((kinds, scen_count)),
             dma((kinds,)),
@@ -645,26 +643,22 @@
 
 def finish_kernel(
     limit,
-    spread,
     place_ref,
-    block_ref,
+    row_label_ref,
+    col_label_ref,
+    lead_label_ref,
+    column_label_ref,
     arrived_ref,
     scales_ref,
-    lead_ref,
-    lead_scales_ref,
-    column_ref,
-    column_scales_ref,
     lower_ref,
-    inverse_ref,
+    side_ref,
+    down_ref,
     diag_ref,
     panel_ref,
     trailing_ref,
     left_ref,
     raw_ref,
-    sums_ref,
     list_ref,
-    row_ref,
-    col_ref,
     count_ref,
 ):
     tile = lower_ref.shape[0]
@@ -673,88 +667,53 @@
     rows_own = diag_ref.shape[0]
     step = pl.program_id(0)
     per_chunk = chunk // tile
-    listed_count = block_ref.shape[0] // lead_ref.shape[0]
     scen, link = place_ref[0], place_ref[1]
     first_col = link * per_chunk * pl.num_programs(0)
 
     @pl.when(step == 0)
     def _():
         raw_ref[...] = jnp.zeros_like(raw_ref)
-
-        @pl.loop(0, lead_ref.shape[0])
+        panel_ref[...] = jnp.zeros_like(panel_ref)
+
+        @pl.loop(0, side_ref.shape[0])
         def _(source):
             for slot in range(slots):
-                block = block_ref[source * listed_count + link * slots + slot] - first_col
-                at = pl.multiple_of(block * tile, tile)
-                raw_ref[:, pl.ds(at, tile)] += (
-                    lead_ref[source, slot].astype(I32).astype(F32)
-                    * lead_scales_ref[source, 0:1, slot * tile : (slot + 1) * tile]
-                )
-
-        sums_ref[...] = jnp.zeros_like(sums_ref)
+                at = pl.multiple_of(lead_label_ref[source * slots + slot] * tile, tile)
+                raw_ref[:, pl.ds(at, tile)] += side_ref[source, slot]
+            for rank in range(limit):
+                label = column_label_ref[source * limit + rank]
+
+                @pl.when(label >= 0)
+                def _():
+                    at = pl.ds(pl.multiple_of(label * tile, tile), tile)
+                    panel_ref[at, :] += down_ref[source, rank * tile : (rank + 1) * tile, :]
+
+        @pl.when(link == 0)
+        def _():
+            raw_ref[:, :tile] = lower_ref[...].T
+
+        @pl.when(scen == 0)
+        def _():
+            panel_ref[:tile, :] = lower_ref[...]
+
+        high, low = split(-panel_ref[...])
+        left_ref[:, :tile] = high
+        left_ref[:, tile : 2 * tile] = low
+        left_ref[:, 2 * tile :] = high
+
         for other in range(count_ref.shape[0]):
             count_ref[other] = 0
 
-        @pl.loop(0, lead_ref.shape[0])
-        def _(source):
-            def visit(listed, rank):
-                row = block_ref[source * listed_count + listed] - scen * rows_own
-                mine = (row >= 0) & (row < rows_own)
-                scenario = source * listed_count + listed // spread * spread
-
-                @pl.when(mine)
-                def _():
-                    for slot in range(slots):
-                        col = block_ref[scenario + link * slots + slot] - first_col
-                        entry = (source * limit + rank) * slots + slot
-                        owner = col // per_chunk
-                        held = count_ref[owner]
-                        list_ref[owner, held] = entry
-                        count_ref[owner] = held + 1
-                        row_ref[entry] = row
-                        col_ref[entry] = col
-
-                @pl.when(mine & (block_ref[scenario] == 0))
-                def _():
-                    scales = column_scales_ref[source, :, :tile]
-                    picked = lax.broadcasted_iota(I32, scales.shape, 0) == rank
-                    scale = jnp.sum(jnp.where(picked, scales, 0.0), axis=0, keepdims=True)
-                    codes = column_ref[source, pl.ds(pl.multiple_of(rank * tile, tile), tile), :]
-                    down = pl.ds(pl.multiple_of(row * tile, tile), tile)
-                    sums_ref[down, :] += codes.astype(I32).astype(F32) * scale
-
-                return rank + mine.astype(I32)
-
-            lax.fori_loop(0, listed_count, visit, jnp.int32(0))
-
-        group = min(4, rows_own) * tile
-        for start in range(0, rows_own * tile, group):
-            at = slice(start, start + group)
-            solved = lax.dot_general(
-                sums_ref[at, :],
-                inverse_ref[...],
-                (((1,), (1,)), ((), ())),
-                precision=HIGHEST,
-                preferred_element_type=F32,
-            )
-            if start == 0:
-                top = jnp.where(scen == 0, lower_ref[...], solved[:tile])
-                solved = jnp.concatenate([top, solved[tile:]], axis=0)
-            panel_ref[at, :] = solved
-            high, low = split(-solved)
-            left_ref[at, :tile] = high
-            left_ref[at, tile : 2 * tile] = low
-            left_ref[at, 2 * tile :] = high
-
-    part = jnp.dot(
-        inverse_ref[...],
-        raw_ref[:, pl.ds(pl.multiple_of(step * chunk, chunk), chunk)],
-        precision=HIGHEST,
-        preferred_element_type=F32,
-    )
-    is_lead = (link == 0) & (step == 0)
-    top = jnp.where(is_lead, lower_ref[...].T, part[:, :tile])
-    part = jnp.concatenate([top, part[:, tile:]], axis=1) if per_chunk > 1 else top
+        @pl.loop(0, list_ref.shape[1])
+        def _(entry):
+            @pl.when(row_label_ref[entry // slots] >= 0)
+            def _():
+                owner = col_label_ref[entry] // per_chunk
+                held = count_ref[owner]
+                list_ref[owner, held] = entry
+                count_ref[owner] = held + 1
+
+    part = raw_ref[:, pl.ds(pl.multiple_of(step * chunk, chunk), chunk)]
     high, low = split(part)
     right = jnp.concatenate([high, high, low], axis=0)
     strip = min(8, rows_own) * tile
@@ -770,8 +729,8 @@
         slot = entry - listed * slots
         source = listed // limit
         rank = listed - source * limit
-        col = col_ref[entry] - step * per_chunk
-        down = pl.ds(pl.multiple_of(row_ref[entry] * tile, tile), tile)
+        col = col_label_ref[entry] - step * per_chunk
+        down = pl.ds(pl.multiple_of(row_label_ref[listed] * tile, tile), tile)
         along = pl.ds(pl.multiple_of(col * tile, tile), tile)
         from_rows = pl.ds(pl.multiple_of(rank * tile, tile), tile)
         from_lanes = pl.ds(pl.multiple_of(slot * tile, tile), tile)
@@ -795,16 +754,16 @@
             )
 
 
-def finish(place, blocks, arrays, spread, limit, width):
-    lower, diag = arrays[6], arrays[8]
-    entries = arrays[0].shape[0] * arrays[0].shape[1] * limit
+def finish(labels, arrays, limit, width):
+    lower, diag = arrays[2], arrays[5]
+    entries = labels[2].shape[0]
     tile = lower.shape[0]
     rows = diag.shape[0] * tile
     chunk = min(512, width)
     return pl.pallas_call(
-        lambda *refs: finish_kernel(limit, spread, *refs),
+        lambda *refs: finish_kernel(limit, *refs),
         grid_spec=pltpu.PrefetchScalarGridSpec(
-            num_scalar_prefetch=2,
+            num_scalar_prefetch=5,
             grid=(width // chunk,),
             in_specs=[VMEM] * len(arrays),
             out_specs=[
@@ -814,10 +773,7 @@
             scratch_shapes=[
                 pltpu.VMEM((rows, 3 * tile), BF16),
                 pltpu.VMEM((tile, width), F32),
-                pltpu.VMEM((rows, tile), F32),
                 pltpu.SMEM((width // chunk, entries), I32),
-                pltpu.SMEM((entries,), I32),
-                pltpu.SMEM((entries,), I32),
                 pltpu.SMEM((width // chunk,), I32),
             ],
         ),
@@ -827,7 +783,7 @@
         ),
         name="finish",
         compiler_params=pltpu.CompilerParams(vmem_limit_bytes=48 * MIB),
-    )(place, blocks, *arrays)
+    )(*labels, *arrays)
 
 
 def per_device(factor_inv, coupling, first_diag, pattern):
@@ -850,18 +806,41 @@
     picks = scen_here * slots
     owners_here = max(1, per_link // rows_own)
     limit = max(1, (picks + owners_here - 1) // owners_here)
+    listed = jnp.arange(scen_here * spread, dtype=I32)
+
+    def targets(blocks):
+        owners = blocks // rows_own
+        earlier = (owners[..., :, None] == owners[..., None, :]) & (
+            listed[None, :] < listed[:, None]
+        )
+        return owners * limit + jnp.sum(earlier.astype(I32), axis=-1)
+
     coded, scales = contribute(
-        pattern.reshape(-1),
-        link_pos[None].astype(I32),
-        gathered,
-        tile,
-        scen_count,
-        rows_own,
-        limit,
+        targets(pattern.reshape(-1)), link_pos[None].astype(I32), gathered, tile, scen_count, limit
     )
+
+    blocks = patterns.reshape(scen_count, scen_here * spread)
+    places = scen_pos * limit + jnp.arange(limit, dtype=I32)
+    hit = targets(blocks)[:, :, None] == places[None, None, :]
+    rows_from = blocks - scen_pos * rows_own + 1
+    row_labels = jnp.sum(jnp.where(hit, rows_from[:, :, None], 0), axis=1) - 1
+    leading = jnp.repeat(patterns[:, :, 0] == 0, spread, axis=1)
+    column_labels = (
+        jnp.sum(jnp.where(hit & leading[:, :, None], rows_from[:, :, None], 0), axis=1) - 1
+    )
+    own_cols = (
+        lax.dynamic_slice_in_dim(patterns, link_pos * slots, slots, 2) - link_pos * per_link
+    )
+    slab_cols = jnp.repeat(own_cols, spread, axis=1)
+    col_labels = jnp.sum(jnp.where(hit[:, :, :, None], slab_cols[:, :, None, :], 0), axis=1)
+    lead_labels = own_cols[:, 0, :]
+
     arrays = exchange(coded, scales, corner, link_count) + (first_diag,)
     place = jnp.stack([scen_pos, link_pos]).astype(I32)
-    return finish(place, patterns.reshape(-1), arrays, spread, limit, per_link * tile)
+    labels = (place,) + tuple(
+        one.reshape(-1) for one in (row_labels, col_labels, lead_labels, column_labels)
+    )
+    return finish(labels, arrays, limit, per_link * tile)
 
 
 def solution(mesh):

time: 114 us -> 108 us (0.947)
  Pallas kernels: 108 us -> 100 us
    pallas_call x2, Pallas kernels: 34.2 us -> 22.2 us  [the longest x1 18.5 us: finish(): pl.pallas_call(lambda *refs: finish_kernel(limit, *refs), grid_spec=pltpu...]
    pallas_call x1, Pallas kernels: 39.1 us -> 43.8 us  [exchange(): pl.pallas_call(lambda *refs: exchange_kernel(scen_count, link_count, *ref...]
where the time goes in v5:
time: 108 us
  Pallas kernels  100 us (93%)
  local copies, waits for them, and re-layouts  5.46 us (5%)
  other arithmetic  1.13 us (1%)
    pallas_call x1, Pallas kernels, exchange(): pl.pallas_call(lambda *refs: exchange_kernel(scen_count, link_count, *ref...  43.8 us
    pallas_call x1, Pallas kernels, gather(): pl.pallas_call(lambda *refs: gather_kernel(scen_count, link_count, *refs)...  34.5 us
    pallas_call x1, Pallas kernels, finish(): pl.pallas_call(lambda *refs: finish_kernel(limit, *refs), grid_spec=pltpu...  18.5 us
    pallas_call x1, Pallas kernels, contribute(): pl.pallas_call(lambda *refs: contribute_kernel(limit, clear, *refs), grid...  3.69 us
    unnamed x8, local copies, waits for them, and re-layouts  2.19 us

profile of v5, /device:TPU:0, one launch (start us, length us, event | category | flops | bytes accessed | tf_op | source)
XLA Modules:
  0.0 107.7 jit_solution(3320896250046858947)
XLA Ops:
  0.7 0.8 reshape.175
  1.5 0.2 convert_reduce_fusion.1
  1.7 1.3 %pad.4.refs_3_ = s32[8,128]{1,0:T(8,128)} pad(s32[2,8]{1,0:T(2,128)} %param.7, s32[]{:T(128)} %constant.40.clone.1), padding=0_6x0_120 | pad | bytes 4164 | tf_op jit(solution)/shard_map/jit(_pad)/pad | solution.py:800
  3.0 34.5 %gather.1 = (bf16[4,2,1024,256]{3,2,1,0:T(8,128)(2,1)}, f32[128,128]{1,0:T(8,128)}, s32[8,8,128]{2,1,0:T(8,128)}) custom-call(bf16[2,1024,1024]{2,1,0:T(8,128)(2,1)} %refs_0_.1, bf16[2,1024,256]{2,1,0:T(8,128)(2,1)} %refs_1_.1, f32[16,128]{1,0:T(8,128)} %refs_10_.1, s32[8,128]{1,0:T(8,128)} %pad.4.refs_3_), custom_call_target="tpu_custom_call" | custom-call | tf_op jit(solution)/shard_map/gather/pallas_call | solution.py:259
  37.5 2.2 %copy-done = bf16[4,2,1024,256]{3,2,1,0:T(8,128)(2,1)S(1)} copy-done((bf16[4,2,1024,256]{3,2,1,0:T(8,128)(2,1)S(1)}, bf16[4,2,1024,256]{3,2,1,0:T(8,128)(2,1)}, u32[]{:S(2)}) %copy-start) | copy-done | bytes 4194328
  39.6 3.7 %contribute.1 = (s16[8,2,256,128]{3,2,1,0:T(8,128)(2,1)S(1)}, f32[8,8,256]{2,1,0:T(8,128)S(1)}) custom-call(s32[16]{0:T(128)S(1)} %multiply_add_fusion.1.refs_0_, s32[1]{0:T(128)} %bitcast.1.refs_1_, bf16[4,2,1024,256]{3,2,1,0:T(8,128)(2,1)S(1)} %copy-done, bf16[4,2,1024,256]{3,2,1,0:T(8,128)(2,1)S(1)} %copy-done), custom_call_target="tpu_custom_call" | custom-call | tf_op jit(solution)/shard_map/contribute/pallas_call | solution.py:326
  43.4 0.1 copy.20
  43.5 0.1 copy.21
  43.6 0.1 reshape.173
  43.8 0.1 reshape_squeeze.3.refs_3_
  43.9 0.1 copy.17
  44.0 0.3 convert_reduce_fusion
  44.3 0.2 select_reduce_fusion.1
  44.6 0.1 copy.22
  44.7 0.1 sub.44.refs_4_
  44.8 0.1 copy.16
  44.9 0.1 sub.40.refs_1_
  44.9 0.1 broadcast_in_dim.62
  45.0 0.1 broadcast_in_dim.63
  45.1 0.2 select_reduce_fusion
  45.3 0.1 copy.18
  45.4 0.1 reshape.174.refs_2_
  45.5 43.8 %exchange.1 = (s16[8,2,256,128]{3,2,1,0:T(8,128)(2,1)S(1)}, f32[8,8,256]{2,1,0:T(8,128)S(1)}, f32[128,128]{1,0:T(8,128)S(1)}, f32[8,2,128,128]{3,2,1,0:T(8,128)S(1)}, f32[8,256,128]{2,1,0:T(8,128)S(1)}) custom-call(s16[8,2,256,128]{3,2,1,0:T(8,128)(2,1)S(1)} %get-tuple-element.14.refs_0_, f32[8,8,256]{2,1,0:T(8,128)S(1)} %get-tuple-element.15.refs_1_, ...), custom_call_target="tpu_custom_call" | custom-call | tf_op jit(solution)/shard_map/exchange/pallas_call | solution.py:607
  89.2 18.5 %finish.1 = (f32[2048,128]{1,0:T(8,128)}, f32[2048,4096]{1,0:T(8,128)}) custom-call(s32[2]{0:T(128)S(1)} %pad_add_fusion.refs_0_, s32[16]{0:T(128)S(1)} %sub.40.refs_1_, s32[32]{0:T(128)S(1)} %reshape.174.refs_2_, s32[16]{0:T(128)S(1)} %reshape_squeeze.3.refs_3_, s32[16]{0:T(128)S(1)} %sub.44.refs_4_, s16[8,2,256,128]{3,2,1,0:T(8,128)(2,1)S(1)} %get-tuple-element.17.refs_5_, ...), custom_call_target="tpu_custom_call" | custom-call | tf_op jit(solution)/shard_map/finish/pallas_call | solution.py:763
  (21 shorter events, 0.3 us)
Async XLA Ops:
  37.5 2.2 %copy-start = (bf16[4,2,1024,256]{3,2,1,0:T(8,128)(2,1)S(1)}, bf16[4,2,1024,256]{3,2,1,0:T(8,128)(2,1)}, u32[]{:S(2)}) copy-start(bf16[4,2,1024,256]{3,2,1,0:T(8,128)(2,1)} %get-tuple-element.13.refs_2_.refs_3_) | copy-start | bytes 12582916
  39.6 3.7 %copy-start.3 = (s32[8,8,128]{2,1,0:T(8,128)S(1)}, s32[8,8,128]{2,1,0:T(8,128)}, u32[]{:S(2)}) copy-start(s32[8,8,128]{2,1,0:T(8,128)} %get-tuple-element.12) | copy-start | bytes 98308
  39.6 5.8 %copy-start.1 = (f32[128,128]{1,0:T(8,128)S(1)}, f32[128,128]{1,0:T(8,128)}, u32[]{:S(2)}) copy-start(f32[128,128]{1,0:T(8,128)} %get-tuple-element.16.refs_2_) | copy-start | bytes 196612
  39.6 49.6 %copy-start.2 = (f32[16,128]{1,0:T(8,128)S(1)}, f32[16,128]{1,0:T(8,128)}, u32[]{:S(2)}) copy-start(f32[16,128]{1,0:T(8,128)} %refs_10_.1) | copy-start | bytes 24580

commit v6 on v5

--- a/solution.py
+++ b/solution.py
@@ -482,15 +482,14 @@
                     lead_wait(block)
                 lead_pass(block, True, False, act)
 
-    over_peers(start_first)
     lead_ref[scen] = coded_ref[0, :, :tile, :]
     lead_scales_ref[scen] = scales_ref[0]
     lead_pass(scen, True, True, begin)
+    over_peers(start_first)
     for kind in first + later:
         keep(kind).start()
     factor_into(corner_ref, lower_ref, inverse_ref)
     over_peers(finish_send(first))
-    over_peers(start_later)
     for kind in first + later:
         keep(kind).wait()
 
@@ -534,6 +533,7 @@
             column_out(peer)
 
     over_line(begin, True)
+    over_peers(start_later)
 
     @pl.when(link == 0)
     def _():

time: 108 us -> 101 us (0.935)
  Pallas kernels: 100 us -> 93.3 us
    pallas_call x1, Pallas kernels: 43.8 us -> 36.5 us  [exchange(): pl.pallas_call(lambda *refs: exchange_kernel(scen_count, link_count, *ref...]
where the time goes in v6:
time: 101 us
  Pallas kernels  93.3 us (92%)
  local copies, waits for them, and re-layouts  5.46 us (5%)
  other arithmetic  1.13 us (1%)
    pallas_call x1, Pallas kernels, exchange(): pl.pallas_call(lambda *refs: exchange_kernel(scen_count, link_count, *ref...  36.5 us
    pallas_call x1, Pallas kernels, gather(): pl.pallas_call(lambda *refs: gather_kernel(scen_count, link_count, *refs)...  34.5 us
    pallas_call x1, Pallas kernels, finish(): pl.pallas_call(lambda *refs: finish_kernel(limit, *refs), grid_spec=pltpu...  18.6 us
    pallas_call x1, Pallas kernels, contribute(): pl.pallas_call(lambda *refs: contribute_kernel(limit, clear, *refs), grid...  3.69 us
    unnamed x8, local copies, waits for them, and re-layouts  2.19 us

profile of v6, /device:TPU:0, one launch (start us, length us, event | category | flops | bytes accessed | tf_op | source)
XLA Modules:
  0.0 100.6 jit_solution(12110302966929899568)
XLA Ops:
  0.7 0.8 reshape.175
  1.5 0.2 convert_reduce_fusion.1
  1.7 1.3 %pad.4.refs_3_ = s32[8,128]{1,0:T(8,128)} pad(s32[2,8]{1,0:T(2,128)} %param.7, s32[]{:T(128)} %constant.40.clone.1), padding=0_6x0_120 | pad | bytes 4164 | tf_op jit(solution)/shard_map/jit(_pad)/pad | solution.py:800
  3.0 34.5 %gather.1 = (bf16[4,2,1024,256]{3,2,1,0:T(8,128)(2,1)}, f32[128,128]{1,0:T(8,128)}, s32[8,8,128]{2,1,0:T(8,128)}) custom-call(bf16[2,1024,1024]{2,1,0:T(8,128)(2,1)} %refs_0_.1, bf16[2,1024,256]{2,1,0:T(8,128)(2,1)} %refs_1_.1, f32[16,128]{1,0:T(8,128)} %refs_10_.1, s32[8,128]{1,0:T(8,128)} %pad.4.refs_3_), custom_call_target="tpu_custom_call" | custom-call | tf_op jit(solution)/shard_map/gather/pallas_call | solution.py:259
  37.5 2.2 %copy-done = bf16[4,2,1024,256]{3,2,1,0:T(8,128)(2,1)S(1)} copy-done((bf16[4,2,1024,256]{3,2,1,0:T(8,128)(2,1)S(1)}, bf16[4,2,1024,256]{3,2,1,0:T(8,128)(2,1)}, u32[]{:S(2)}) %copy-start) | copy-done | bytes 4194328
  39.6 3.7 %contribute.1 = (s16[8,2,256,128]{3,2,1,0:T(8,128)(2,1)S(1)}, f32[8,8,256]{2,1,0:T(8,128)S(1)}) custom-call(s32[16]{0:T(128)S(1)} %multiply_add_fusion.1.refs_0_, s32[1]{0:T(128)} %bitcast.1.refs_1_, bf16[4,2,1024,256]{3,2,1,0:T(8,128)(2,1)S(1)} %copy-done, bf16[4,2,1024,256]{3,2,1,0:T(8,128)(2,1)S(1)} %copy-done), custom_call_target="tpu_custom_call" | custom-call | tf_op jit(solution)/shard_map/contribute/pallas_call | solution.py:326
  43.4 0.1 copy.20
  43.5 0.1 copy.21
  43.6 0.1 reshape.173
  43.8 0.1 reshape_squeeze.3.refs_3_
  43.9 0.1 copy.17
  44.0 0.3 convert_reduce_fusion
  44.3 0.2 select_reduce_fusion.1
  44.6 0.1 copy.22
  44.7 0.1 sub.44.refs_4_
  44.8 0.1 copy.16
  44.9 0.1 sub.40.refs_1_
  44.9 0.1 broadcast_in_dim.62
  45.0 0.1 broadcast_in_dim.63
  45.1 0.2 select_reduce_fusion
  45.3 0.1 copy.18
  45.4 0.1 reshape.174.refs_2_
  45.5 36.5 %exchange.1 = (s16[8,2,256,128]{3,2,1,0:T(8,128)(2,1)S(1)}, f32[8,8,256]{2,1,0:T(8,128)S(1)}, f32[128,128]{1,0:T(8,128)S(1)}, f32[8,2,128,128]{3,2,1,0:T(8,128)S(1)}, f32[8,256,128]{2,1,0:T(8,128)S(1)}) custom-call(s16[8,2,256,128]{3,2,1,0:T(8,128)(2,1)S(1)} %get-tuple-element.14.refs_0_, f32[8,8,256]{2,1,0:T(8,128)S(1)} %get-tuple-element.15.refs_1_, ...), custom_call_target="tpu_custom_call" | custom-call | tf_op jit(solution)/shard_map/exchange/pallas_call | solution.py:607
  82.0 18.6 %finish.1 = (f32[2048,128]{1,0:T(8,128)}, f32[2048,4096]{1,0:T(8,128)}) custom-call(s32[2]{0:T(128)S(1)} %pad_add_fusion.refs_0_, s32[16]{0:T(128)S(1)} %sub.40.refs_1_, s32[32]{0:T(128)S(1)} %reshape.174.refs_2_, s32[16]{0:T(128)S(1)} %reshape_squeeze.3.refs_3_, s32[16]{0:T(128)S(1)} %sub.44.refs_4_, s16[8,2,256,128]{3,2,1,0:T(8,128)(2,1)S(1)} %get-tuple-element.17.refs_5_, ...), custom_call_target="tpu_custom_call" | custom-call | tf_op jit(solution)/shard_map/finish/pallas_call | solution.py:763
  (21 shorter events, 0.3 us)
Async XLA Ops:
  37.5 2.2 %copy-start = (bf16[4,2,1024,256]{3,2,1,0:T(8,128)(2,1)S(1)}, bf16[4,2,1024,256]{3,2,1,0:T(8,128)(2,1)}, u32[]{:S(2)}) copy-start(bf16[4,2,1024,256]{3,2,1,0:T(8,128)(2,1)} %get-tuple-element.13.refs_2_.refs_3_) | copy-start | bytes 12582916
  39.6 3.7 %copy-start.3 = (s32[8,8,128]{2,1,0:T(8,128)S(1)}, s32[8,8,128]{2,1,0:T(8,128)}, u32[]{:S(2)}) copy-start(s32[8,8,128]{2,1,0:T(8,128)} %get-tuple-element.12) | copy-start | bytes 98308
  39.6 5.8 %copy-start.1 = (f32[128,128]{1,0:T(8,128)S(1)}, f32[128,128]{1,0:T(8,128)}, u32[]{:S(2)}) copy-start(f32[128,128]{1,0:T(8,128)} %get-tuple-element.16.refs_2_) | copy-start | bytes 196612
  39.6 42.4 %copy-start.2 = (f32[16,128]{1,0:T(8,128)S(1)}, f32[16,128]{1,0:T(8,128)}, u32[]{:S(2)}) copy-start(f32[16,128]{1,0:T(8,128)} %refs_10_.1) | copy-start | bytes 24580
